TPU v7x, 256 devices: a whole 4x4x8 slice. The times are simulated.
256 devices in a mesh: frame: 32 (over x_lo, z, core), quad: 8 (over x_hi, y).
Axes of the slice: x: 4 (x_hi: 2, x_lo: 2; x = x_hi * 2 + x_lo), y: 4, z: 8, core: 2. Of those that a mesh axis runs over, the one named last changes fastest.
Arguments:
- activations: bfloat16 [128, 256, 1280], P('frame', 'quad'), may hold values from -48 to 48
- cotangent: bfloat16 [128, 256, 1280], P('frame', 'quad'), may hold values from -6 to 6
- spatial_weights: bfloat16 [4, 1280, 640], replicated, may hold values from -2 to 2
- spatial_gain: float32 [1280], replicated, may hold values from 0.1 to 1.9
- motion_weights: bfloat16 [4, 1280, 640], P(None, 'quad'), may hold values from -2 to 2
- motion_gain: float32 [1280], replicated, may hold values from 0.1 to 1.9
Outputs:
- block_output: bfloat16 [128, 256, 1280], P('frame', 'quad')
- input_grad: bfloat16 [128, 256, 1280], P('frame', 'quad')
- weight_grad: float32 [4, 1280, 640], P(None, ('frame', 'quad'))
- gain_grad: float32 [1280], P(('frame', 'quad'))
All inputs are finite; a program needn't handle non-finite values.
Results may differ from a plain program's by a relative error of at most 0.03.
Values may be sent and summed in bfloat16 or wider, within the bound.
A program may use at most 128 MiB of HBM per device.

v0:
```python
import math

import jax
import jax.numpy as jnp
from jax import lax
from jax.sharding import PartitionSpec as P

HEADS = 4
HEAD_DIM = 160


EPSILON = 1e-05


def normalize(values, gain):
    average = jnp.mean(values, axis=-1, keepdims=True)
    centred = values - average
    inv_scale = lax.rsqrt(jnp.mean(centred * centred, axis=-1, keepdims=True) + EPSILON)
    unit_rows = centred * inv_scale
    return (unit_rows * gain, unit_rows, inv_scale)


def normalize_back(grad_rows, unit_rows, inv_scale, gain):
    scaled = grad_rows * gain
    first_mean = jnp.mean(scaled, axis=-1, keepdims=True)
    second_mean = jnp.mean(scaled * unit_rows, axis=-1, keepdims=True)
    return inv_scale * (scaled - first_mean - unit_rows * second_mean)


def positional(frames, channels):
    frame_pos = jnp.arange(frames).astype(jnp.float32)[:, None]
    freq_index = jnp.arange(channels // 2).astype(jnp.float32)[None, :]
    phases = frame_pos * jnp.exp(freq_index * (-2.0 * math.log(10000.0) / channels))
    return jnp.stack([jnp.sin(phases), jnp.cos(phases)], axis=-1).reshape(frames, channels)


def project(row_block, weight):
    flattened = row_block.reshape(-1, row_block.shape[-1])
    result = jnp.dot(flattened, weight, preferred_element_type=jnp.float32)
    return result.reshape(row_block.shape[:-1] + (weight.shape[-1],))


def project_back(row_block, weight):
    flattened = row_block.reshape(-1, row_block.shape[-1])
    result = jnp.dot(flattened, weight.T, preferred_element_type=jnp.float32)
    return result.reshape(row_block.shape[:-1] + (weight.shape[0],))


def outer_sum(left_rows, right_rows):
    left_flat = left_rows.reshape(-1, left_rows.shape[-1])
    right_flat = right_rows.reshape(-1, right_rows.shape[-1])
    return jnp.dot(left_flat.T, right_flat, preferred_element_type=jnp.float32)


def split_heads(tensor):
    return tensor.reshape(tensor.shape[:-1] + (HEADS, HEAD_DIM))


def attend(queries, key_rows, value_rows):
    query_heads = split_heads(queries)
    key_heads = split_heads(key_rows)
    value_heads = split_heads(value_rows)
    scores = jnp.einsum(
        "bqhd,bkhd->bhqk", query_heads, key_heads, preferred_element_type=jnp.float32
    ) * HEAD_DIM ** (-0.5)
    highest = jnp.max(scores, axis=-1, keepdims=True)
    expo_rows = jnp.exp(scores - highest)
    probs = (expo_rows / jnp.sum(expo_rows, axis=-1, keepdims=True)).astype(jnp.bfloat16)
    result = jnp.einsum("bhqk,bkhd->bqhd", probs, value_heads, preferred_element_type=jnp.float32)
    return result.reshape(queries.shape).astype(jnp.bfloat16)


def score_grads(queries, key_rows, value_rows, grad_rows):
    query_heads = split_heads(queries)
    key_heads = split_heads(key_rows)
    value_heads = split_heads(value_rows)
    grad_heads = split_heads(grad_rows)
    scores = jnp.einsum(
        "bqhd,bkhd->bhqk", query_heads, key_heads, preferred_element_type=jnp.float32
    ) * HEAD_DIM ** (-0.5)
    highest = jnp.max(scores, axis=-1, keepdims=True)
    log_total = highest + jnp.log(jnp.sum(jnp.exp(scores - highest), axis=-1, keepdims=True))
    probs = jnp.exp(scores - log_total)
    grad_probs = jnp.einsum(
        "bqhd,bkhd->bhqk", grad_heads, value_heads, preferred_element_type=jnp.float32
    )
    inner_sum = jnp.sum(probs * grad_probs, axis=-1, keepdims=True)
    grad_scores = (probs * (grad_probs - inner_sum) * HEAD_DIM ** (-0.5)).astype(jnp.bfloat16)
    return (probs.astype(jnp.bfloat16), grad_scores)


def attend_back(queries, key_rows, value_rows, grad_rows):
    probs, grad_scores = score_grads(queries, key_rows, value_rows, grad_rows)
    query_heads = split_heads(queries)
    key_heads = split_heads(key_rows)
    grad_heads = split_heads(grad_rows)
    grad_query = jnp.einsum(
        "bhqk,bkhd->bqhd", grad_scores, key_heads, preferred_element_type=jnp.float32
    )
    grad_key = jnp.einsum(
        "bhqk,bqhd->bkhd", grad_scores, query_heads, preferred_element_type=jnp.float32
    )
    grad_value = jnp.einsum(
        "bhqk,bqhd->bkhd", probs, grad_heads, preferred_element_type=jnp.float32
    )
    return (
        grad_query.reshape(queries.shape).astype(jnp.bfloat16),
        grad_key.reshape(key_rows.shape).astype(jnp.bfloat16),
        grad_value.reshape(key_rows.shape).astype(jnp.bfloat16),
    )


def to_positions(values):
    return lax.all_to_all(values, "frame", split_axis=1, concat_axis=0, tiled=True)


def to_frames(values):
    return lax.all_to_all(values, "frame", split_axis=0, concat_axis=1, tiled=True)


def local(activations, cotangent, spatial_weights, spatial_gain, motion_weights, motion_gain):
    frames_dev, cells_dev, channels = activations.shape
    grad_cells = to_positions(cotangent)
    input_wide = activations.astype(jnp.float32)
    normed, unit_one, scale_one = normalize(input_wide, spatial_gain)
    normed_one = normed.astype(jnp.bfloat16)
    spatial_query = project(normed_one, spatial_weights[0]).astype(jnp.bfloat16)
    spatial_keys = project(normed_one, spatial_weights[1]).astype(jnp.bfloat16)
    spatial_values = project(normed_one, spatial_weights[2]).astype(jnp.bfloat16)
    keys_all, values_all, motion_full = (
        lax.all_gather(spatial_keys, "quad", axis=1, tiled=True),
        lax.all_gather(spatial_values, "quad", axis=1, tiled=True),
        lax.all_gather(motion_weights, "quad", axis=1, tiled=True),
    )
    spatial_out = attend(spatial_query, keys_all, values_all)
    hidden = (input_wide + project_back(spatial_out, spatial_weights[3])).astype(jnp.bfloat16)
    hidden_cells = to_positions(hidden)
    by_cell = jnp.swapaxes(hidden_cells, 0, 1)
    cell_wide = by_cell.astype(jnp.float32)
    normed_t, unit_two, scale_two = normalize(cell_wide, motion_gain)
    normed_two = (normed_t + positional(by_cell.shape[1], channels)[None]).astype(jnp.bfloat16)
    motion_query = project(normed_two, motion_full[0]).astype(jnp.bfloat16)
    motion_keys = project(normed_two, motion_full[1]).astype(jnp.bfloat16)
    motion_values = project(normed_two, motion_full[2]).astype(jnp.bfloat16)
    motion_out = attend(motion_query, motion_keys, motion_values)
    result_cells = (cell_wide + project_back(motion_out, motion_full[3])).astype(jnp.bfloat16)
    result_frames = jnp.swapaxes(result_cells, 0, 1)
    block_output = to_frames(result_frames)
    grad_by_cell = jnp.swapaxes(grad_cells, 0, 1)
    grad_motion_out = project(grad_by_cell, motion_full[3]).astype(jnp.bfloat16)
    grad_out_proj = outer_sum(grad_by_cell, motion_out)
    grad_mq, grad_mk, grad_mv = attend_back(
        motion_query, motion_keys, motion_values, grad_motion_out
    )
    weight_terms = jnp.stack(
        [
            outer_sum(normed_two, grad_mq),
            outer_sum(normed_two, grad_mk),
            outer_sum(normed_two, grad_mv),
            grad_out_proj,
        ]
    )
    grad_normed_two = (
        project_back(grad_mq, motion_full[0])
        + project_back(grad_mk, motion_full[1])
        + project_back(grad_mv, motion_full[2])
    )
    gain_terms = jnp.sum((grad_normed_two * unit_two).reshape(-1, channels), axis=0)
    weight_share, gain_share = (
        lax.psum_scatter(weight_terms, ("frame", "quad"), scatter_dimension=1, tiled=True),
        lax.psum_scatter(gain_terms, ("frame", "quad"), scatter_dimension=0, tiled=True),
    )
    grad_hidden_cells = (
        grad_by_cell.astype(jnp.float32)
        + normalize_back(grad_normed_two, unit_two, scale_two, motion_gain)
    ).astype(jnp.bfloat16)
    grad_hidden_frames = jnp.swapaxes(grad_hidden_cells, 0, 1)
    grad_hidden = to_frames(grad_hidden_frames)
    grad_spatial_out = project(grad_hidden, spatial_weights[3]).astype(jnp.bfloat16)
    probs, grad_scores = score_grads(spatial_query, keys_all, values_all, grad_spatial_out)
    grad_sq = (
        jnp.einsum(
            "bhqk,bkhd->bqhd",
            grad_scores,
            split_heads(keys_all),
            preferred_element_type=jnp.float32,
        )
        .reshape(spatial_query.shape)
        .astype(jnp.bfloat16)
    )
    key_terms = jnp.einsum(
        "bhqk,bqhd->bkhd",
        grad_scores,
        split_heads(spatial_query),
        preferred_element_type=jnp.float32,
    ).reshape(keys_all.shape)
    value_terms = jnp.einsum(
        "bhqk,bqhd->bkhd", probs, split_heads(grad_spatial_out), preferred_element_type=jnp.float32
    ).reshape(keys_all.shape)
    key_sum, value_sum = (
        lax.psum_scatter(
            key_terms.astype(jnp.bfloat16), "quad", scatter_dimension=1, tiled=True
        ).astype(jnp.float32),
        lax.psum_scatter(
            value_terms.astype(jnp.bfloat16), "quad", scatter_dimension=1, tiled=True
        ).astype(jnp.float32),
    )
    grad_sk = key_sum.astype(jnp.bfloat16)
    grad_sv = value_sum.astype(jnp.bfloat16)
    grad_normed_one = (
        project_back(grad_sq, spatial_weights[0])
        + project_back(grad_sk, spatial_weights[1])
        + project_back(grad_sv, spatial_weights[2])
    )
    input_grad = (
        grad_hidden.astype(jnp.float32)
        + normalize_back(grad_normed_one, unit_one, scale_one, spatial_gain)
    ).astype(jnp.bfloat16)
    tokens_all = frames_dev * lax.axis_size("frame") * cells_dev * lax.axis_size("quad")
    factor = 1.0 / math.sqrt(tokens_all)
    return (block_output, input_grad, weight_share * factor, gain_share * factor)


def solution(mesh):
    in_specs = (
        P("frame", "quad", None),
        P("frame", "quad", None),
        P(),
        P(),
        P(None, "quad", None),
        P(),
    )
    out_specs = (
        P("frame", "quad", None),
        P("frame", "quad", None),
        P(None, ("frame", "quad"), None),
        P(("frame", "quad")),
    )
    return jax.shard_map(local, mesh=mesh, in_specs=in_specs, out_specs=out_specs, check_vma=False)
```

profile of v0, /device:TPU:1, one launch (start us, length us, event | category | flops | bytes accessed | tf_op | source)
XLA Modules:
  0.0 756.1 jit_solution(13723202638851523701)
XLA Ops:
  9.6 2.7 fusion.45
  12.5 2.6 fusion.51
  16.8 11.1 %all-to-all-start.2 = ((bf16[4,32,1280]{2,0,1:T(4,128)(2,1)}), bf16[4,32,1280]{2,0,1:T(4,128)(2,1)S(1)}, u32[]{:S(2)}, u32[]{:S(2)}) async-start(bf16[4,32,1280]{2,0,1:T(4,128)(2,1)} %copy.144), calls=%async_computation.2 | async-start | bytes 655360 | tf_op jit(solution)/shard_map/all_to_all | solution.py:114
  27.8 1.9 fusion.48
  30.0 39.5 %all-gather.4.cloned.1.call-done = bf16[4,256,640]{2,1,0:T(8,128)(2,1)} async-done(((bf16[4,32,640]{2,1,0:T(8,128)(2,1)}), bf16[4,256,640]{2,1,0:T(8,128)(2,1)}) %all-gather.4.cloned.1.call-update) | async-done | bytes 1310736 | tf_op jit(solution)/shard_map/all_gather | solution.py:132
  69.5 2.4 copy.128
  72.0 52.0 %all-gather.6.cloned.1.call-done = bf16[4,256,640]{2,1,0:T(8,128)(2,1)} async-done(((bf16[4,32,640]{2,1,0:T(8,128)(2,1)}), bf16[4,256,640]{2,1,0:T(8,128)(2,1)}) %all-gather.6.cloned.1.call-update) | async-done | bytes 1310736 | tf_op jit(solution)/shard_map/all_gather | solution.py:131
  128.6 2.0 fusion.3
  131.6 9.5 %all-to-all-start = ((bf16[4,32,1280]{2,0,1:T(4,128)(2,1)}), bf16[4,32,1280]{2,0,1:T(4,128)(2,1)S(1)}, u32[]{:S(2)}, u32[]{:S(2)}) async-start(bf16[4,32,1280]{2,0,1:T(4,128)(2,1)} %copy.132), calls=%async_computation | async-start | bytes 655360 | tf_op jit(solution)/shard_map/all_to_all | solution.py:114
  141.6 2.1 multiply_sine_fusion
  143.7 10.3 %all-to-all-done = bf16[4,32,1280]{2,0,1:T(4,128)(2,1)S(1)} async-done(((bf16[4,32,1280]{2,0,1:T(4,128)(2,1)}), bf16[4,32,1280]{2,0,1:T(4,128)(2,1)S(1)}, u32[]{:S(2)}, u32[]{:S(2)}) %all-to-all-start) | async-done | bytes 327712 | tf_op jit(solution)/shard_map/all_to_all | solution.py:114
  155.0 10.7 %copy.133 = f32[32,4,1,1280]{1,0,3,2:T(8,128)} copy(f32[32,4,1,1280]{3,1,0,2:T(4,128)S(1)} %convert_bitcast_fusion) | data formatting | bytes 1310720 | tf_op jit(solution)/shard_map/convert_element_type | solution.py:139
  167.4 19.9 %reshape.849 = f32[128,640,2]{0,2,1:T(2,128)} reshape(f32[32,4,1,1280]{1,0,3,2:T(8,128)} %copy.133) | data formatting | bytes 1310720 | tf_op jit(solution)/shard_map/convert_element_type | solution.py:139
  187.2 2.1 copy.136
  189.8 3.1 multiply_reduce_fusion.3
  192.9 2.1 fusion.74
  195.0 1.9 copy.138
  196.9 28.8 %all-gather.8.cloned.1.call-done = bf16[4,1280,640]{2,1,0:T(8,128)(2,1)} async-done(((bf16[4,160,640]{2,1,0:T(8,128)(2,1)}), bf16[4,1280,640]{2,1,0:T(8,128)(2,1)}) %all-gather.8.cloned.1.call-update) | async-done | bytes 6553616 | tf_op jit(solution)/shard_map/all_gather | solution.py:133
  228.5 1.9 fusion.43
  237.9 2.0 fusion.125
  239.9 2.0 convolution_convert_fusion.6
  241.9 2.0 convolution_convert_fusion.5
  245.1 2.2 fusion.20
  247.2 2.1 convolution_add_fusion.3
  249.4 2.2 multiply_reduce_fusion.1
  253.2 2.5 reduce.19
  255.6 1.9 reshape.862
  257.5 8.3 %all-to-all-start.3 = ((bf16[32,2,2560]{2,1,0:T(2,128)(2,1)}), bf16[32,2,2560]{2,1,0:T(2,128)(2,1)}, u32[]{:S(2)}, u32[]{:S(2)}) async-start(bf16[32,2,2560]{2,1,0:T(2,128)(2,1)} %reshape.862), calls=%async_computation.3 | async-start | bytes 655360 | tf_op jit(solution)/shard_map/all_to_all | solution.py:118
  265.9 13.0 %all-to-all-done.3 = bf16[32,2,2560]{2,1,0:T(2,128)(2,1)} async-done(((bf16[32,2,2560]{2,1,0:T(2,128)(2,1)}), bf16[32,2,2560]{2,1,0:T(2,128)(2,1)}, u32[]{:S(2)}, u32[]{:S(2)}) %all-to-all-start.3) | async-done | bytes 327712 | tf_op jit(solution)/shard_map/all_to_all | solution.py:118
  278.9 3.2 reshape.863
  282.1 3.6 reduce.17
  287.5 2.6 fusion.54
  292.0 2.5 fusion.96
  294.5 5.2 convolution_convert_fusion.1
  299.7 2.4 copy.154
  302.3 2.6 convolution_convert_fusion
  304.9 2.4 copy.156
  312.2 19.5 %copy.158 = f32[4,1280,640]{2,0,1:T(4,128)} copy(f32[4,1280,640]{2,1,0:T(8,128)S(1)} %pad_maximum_fusion) | data formatting | bytes 26214400 | tf_op jit(solution)/shard_map/stack | solution.py:155
  332.6 2.0 fusion.5
  336.4 5.4 all-to-all-start.1
  341.8 76.5 %all-reduce.1 = f32[1280]{0:T(1024)S(1)} all-reduce(f32[1280]{0:T(1024)S(1)} %get-tuple-element.20), channel_id=5, replica_groups=mesh['frame'=32,'quad'=8] {'frame','quad'}, use_global_device_ids=true, to_apply=%region_18.0.clone | all-reduce | flops 1280 | bytes 10240
  419.1 1.9 reduce.16
  421.9 3.7 fusion.40
  426.1 2.0 fusion.12
  428.1 2.2 convolution_add_fusion.1
  430.3 24.7 %reduce-scatter.5.cloned.1.call-done = bf16[4,32,640]{2,1,0:T(8,128)(2,1)} async-done(((bf16[4,256,640]{2,1,0:T(8,128)(2,1)}), bf16[4,32,640]{2,1,0:T(8,128)(2,1)}) %reduce-scatter.5.cloned.1.call-update) | async-done | bytes 163856 | tf_op jit(solution)/shard_map/reduce_scatter | solution.py:204
  455.0 2.2 fusion.122
  458.3 289.2 %all-reduce.4.cloned.1.call-done = f32[4,1280,640]{2,0,1:T(4,128)} async-done(((f32[4,1280,640]{2,0,1:T(4,128)}), f32[4,1280,640]{2,0,1:T(4,128)}) %all-reduce.4.cloned.1.call-update) | async-done | bytes 13107216
  (109 shorter events, 42.2 us)
Async XLA Ops:
  7.2 5.3 copy-start
  7.2 5.3 copy-start.15
  7.2 62.4 %all-gather.4.cloned.1.call-start = ((), (), s32[]{:S(2)}) async-start(), calls=%async_computation.6 | async-start | bytes 1474560 | tf_op jit(solution)/shard_map/all_gather | solution.py:132
  9.6 6.2 copy-start.13
  12.4 111.6 %all-gather.6.cloned.1.call-start = ((), (), s32[]{:S(2)}) async-start(), calls=%async_computation.7 | async-start | bytes 1474560 | tf_op jit(solution)/shard_map/all_gather | solution.py:131
  15.1 210.7 %all-gather.8.cloned.1.call-start = ((), (), s32[]{:S(2)}) async-start(), calls=%async_computation.8 | async-start | bytes 7372800 | tf_op jit(solution)/shard_map/all_gather | solution.py:133
  16.8 114.9 %all-to-all-start.2 = ((bf16[4,32,1280]{2,0,1:T(4,128)(2,1)}), bf16[4,32,1280]{2,0,1:T(4,128)(2,1)S(1)}, u32[]{:S(2)}, u32[]{:S(2)}) async-start(bf16[4,32,1280]{2,0,1:T(4,128)(2,1)} %copy.144), calls=%async_computation.2 | async-start | bytes 655360 | tf_op jit(solution)/shard_map/all_to_all | solution.py:114
  30.0 96.0 %copy-start.4 = (bf16[4,32,4,160]{3,2,1,0:T(4,128)(2,1)}, bf16[4,32,4,160]{3,2,1,0:T(4,128)(2,1)S(1)}, u32[]{:S(2)}) copy-start(bf16[4,32,4,160]{3,2,1,0:T(4,128)(2,1)S(1)} %reshape.841) | copy-start | bytes 491524
  128.2 13.0 %copy-start.14 = (f32[1280]{0:T(1024)S(1)}, f32[1280]{0:T(1024)}, u32[]{:S(2)}) copy-start(f32[1280]{0:T(1024)} %param.11) | copy-start | bytes 15364
  131.6 22.4 %all-to-all-start = ((bf16[4,32,1280]{2,0,1:T(4,128)(2,1)}), bf16[4,32,1280]{2,0,1:T(4,128)(2,1)S(1)}, u32[]{:S(2)}, u32[]{:S(2)}) async-start(bf16[4,32,1280]{2,0,1:T(4,128)(2,1)} %copy.132), calls=%async_computation | async-start | bytes 655360 | tf_op jit(solution)/shard_map/all_to_all | solution.py:114
  154.0 0.7 copy-start.2
  167.4 21.9 %copy-start.3 = (bf16[4,32,1280]{2,0,1:T(4,128)(2,1)S(1)}, bf16[4,32,1280]{2,0,1:T(4,128)(2,1)}, u32[]{:S(2)}) copy-start(bf16[4,32,1280]{2,0,1:T(4,128)(2,1)} %copy-done.2) | copy-start | bytes 983044
  167.4 25.5 %copy-start.7 = (f32[128,640,1]{1,0,2:T(8,128)S(1)}, f32[128,640,1]{1,0,2:T(8,128)}, u32[]{:S(2)}) copy-start(f32[128,640,1]{1,0,2:T(8,128)} %get-tuple-element.25) | copy-start | bytes 983044
  245.1 6.5 copy-start.5
  257.5 21.3 %all-to-all-start.3 = ((bf16[32,2,2560]{2,1,0:T(2,128)(2,1)}), bf16[32,2,2560]{2,1,0:T(2,128)(2,1)}, u32[]{:S(2)}, u32[]{:S(2)}) async-start(bf16[32,2,2560]{2,1,0:T(2,128)(2,1)} %reshape.862), calls=%async_computation.3 | async-start | bytes 655360 | tf_op jit(solution)/shard_map/all_to_all | solution.py:118
  265.9 162.3 %reduce-scatter.3.cloned.1.call-start = ((), (), s32[]{:S(2)}) async-start(), calls=%async_computation.9 | async-start | bytes 1474560 | tf_op jit(solution)/shard_map/reduce_scatter | solution.py:201
  302.2 152.8 %reduce-scatter.5.cloned.1.call-start = ((), (), s32[]{:S(2)}) async-start(), calls=%async_computation.10 | async-start | bytes 1474560 | tf_op jit(solution)/shard_map/reduce_scatter | solution.py:204
  307.4 440.2 %all-reduce.4.cloned.1.call-start = ((), (), s32[]{:S(2)}) async-start(), calls=%async_computation.11 | async-start | bytes 26214400
  307.6 1.6 copy-start.9
  307.6 2.2 copy-start.8
  309.2 1.2 copy-start.12
  310.6 1.6 copy-start.10
  331.7 0.9 copy-start.11
  336.4 82.5 %all-to-all-start.1 = ((bf16[32,2,2560]{2,1,0:T(2,128)(2,1)}), bf16[32,2,2560]{2,1,0:T(2,128)(2,1)S(1)}, u32[]{:S(2)}, u32[]{:S(2)}) async-start(bf16[32,2,2560]{2,1,0:T(2,128)(2,1)} %reshape.860), calls=%async_computation.1 | async-start | bytes 655360 | tf_op jit(solution)/shard_map/all_to_all | solution.py:118
  425.6 29.4 %copy-start.1 = (bf16[4,32,1280]{2,1,0:T(8,128)(2,1)S(1)}, bf16[4,32,1280]{2,1,0:T(8,128)(2,1)}, u32[]{:S(2)}) copy-start(bf16[4,32,1280]{2,1,0:T(8,128)(2,1)} %param.6) | copy-start | bytes 983044
  428.1 29.2 %copy-start.6 = (bf16[32,4,1,1280]{3,1,0,2:T(4,128)(2,1)S(1)}, bf16[32,4,1,1280]{3,1,0,2:T(4,128)(2,1)}, u32[]{:S(2)}) copy-start(bf16[32,4,1,1280]{3,1,0,2:T(4,128)(2,1)} %all_to_all.53) | copy-start | bytes 983044
Sparse Core Ops, SparseCore 0:
  12.5 56.9 all-gather.3
  72.1 51.8 all-gather.5
  126.6 99.0 all-gather.7
  302.3 71.8 reduce-scatter.2
  378.0 76.9 reduce-scatter.4
  460.5 286.9 all-reduce.3
where the time goes:
time: 763 us; the launch traced here: 756 us
  waiting for transfers between devices  458 us (60%)
  local copies, waits for them, and re-layouts  84.7 us (11%)
  blocking collectives  76.5 us (10%)
  matrix products  62.7 us (8%)
  starting transfers between devices  34.7 us (5%)
  other arithmetic  24.2 us (3%)
  between operations  14.9 us (2%)
    unnamed x7, waiting for transfers between devices  290 us
    unnamed x1, blocking collectives  76.5 us
    all_gather x1, waiting for transfers between devices, local(): lax.all_gather(spatial_keys, 'quad', axis=1, tiled=True)  52 us
    all_gather x1, waiting for transfers between devices, local(): lax.all_gather(spatial_values, 'quad', axis=1, tiled=True)  39.5 us
    convert_element_type x5, local copies, waits for them, and re-layouts, local(): cell_wide = by_cell.astype(jnp.float32)  34.5 us
    all_gather x1, waiting for transfers between devices, local(): lax.all_gather(motion_weights, 'quad', axis=1, tiled=True)  28.8 us
    reduce_scatter x1, waiting for transfers between devices, local(): lax.psum_scatter(value_terms.astype(jnp.bfloat16), 'quad', scatter_dimens...  24.7 us
    all_to_all x2, starting transfers between devices, to_positions(): lax.all_to_all(values, 'frame', split_axis=1, concat_axis=0, tiled=True)  20.6 us
  transfers between devices with their start and end apart: 10, of which 7 were waited for; matrix products, arithmetic and copies ran while one was open for 14% of the time, Pallas kernels for 0%

commit v1 on v0

v1 whole, which is shorter than its diff:
```python
import math

import jax
import jax.numpy as jnp
import numpy as np
from jax import lax
from jax.experimental import pallas as pl
from jax.experimental.pallas import tpu as pltpu
from jax.sharding import PartitionSpec as P

HEADS = 4
HEAD_DIM = 160
EPSILON = 1e-05
SCALE = HEAD_DIM ** (-0.5)
C = 1280
W = 640
F32 = jnp.float32
BF = jnp.bfloat16
MESH = pl.DeviceIdType.MESH


def nn(a, b):
    return jnp.dot(a, b, preferred_element_type=F32)


def nt(a, b):
    return lax.dot_general(a, b, (((1,), (1,)), ((), ())), preferred_element_type=F32)


def tn(a, b):
    return lax.dot_general(a, b, (((0,), (0,)), ((), ())), preferred_element_type=F32)


def unit(x):
    xc = x - jnp.mean(x, axis=-1, keepdims=True)
    r = lax.rsqrt(jnp.mean(xc * xc, axis=-1, keepdims=True) + EPSILON)
    return xc * r, r


def unit_back(grad, u, r, gain):
    g = grad * gain
    return r * (g - jnp.mean(g, axis=-1, keepdims=True) - u * jnp.mean(g * u, axis=-1, keepdims=True))


def head_of(x, h):
    lane = lax.broadcasted_iota(jnp.int32, x.shape, 1)
    return jnp.where((lane >= h * HEAD_DIM) & (lane < (h + 1) * HEAD_DIM), x, jnp.zeros_like(x))


def split_pair(y):
    return y[:, :384], pltpu.roll(y, 320, 1)[:, :384]


def join_pair(a, b):
    pad = jnp.zeros((a.shape[0], 256), F32)
    left = jnp.concatenate([a, pad], axis=1)
    right = pltpu.roll(jnp.concatenate([b, pad], axis=1), 320, 1)
    lane = lax.broadcasted_iota(jnp.int32, left.shape, 1)
    return jnp.where(lane < 320, left, right)


def row_order():
    row = lax.broadcasted_iota(jnp.int32, (128, 128), 0)
    col = lax.broadcasted_iota(jnp.int32, (128, 128), 1)
    return jnp.where(col == (row % 4) * 32 + row // 4, 1.0, 0.0).astype(BF)


def scatter_rows(to, rows):
    for n in range(32):
        to[n] = rows[4 * n:4 * n + 4, :].astype(BF)


def gather_rows(rows, come):
    for n in range(32):
        rows[4 * n:4 * n + 4, :] = come[n].astype(F32)


def softmax(q, k):
    s = nt(q, k) * SCALE
    e = jnp.exp(s - jnp.max(s, axis=-1, keepdims=True))
    return e / jnp.sum(e, axis=-1, keepdims=True)


def attend_back(q, k, v, g, probs, heads):
    dq = dk = dv = None
    for h in range(heads):
        r = probs[h]
        dr = nt(head_of(g, h), v)
        delta = jnp.sum(r * dr, axis=-1, keepdims=True)
        ds = (r * (dr - delta) * SCALE).astype(BF)
        a, b, c = nn(ds, head_of(k, h)), tn(ds, head_of(q, h)), tn(r.astype(BF), head_of(g, h))
        dq, dk, dv = (a, b, c) if dq is None else (dq + a, dk + b, dv + c)
    return dq, dk, dv


def kernel(act_h, cot_h, spw_h, spg, mw_h, mgn, pe_h, perm_h,
           bo, ig, wg, gn,
           act, cot, spw, mw, pe, perm,
           qkv_s, qkv_r, o_s, o_r, prob_s,
           hid, hid_s, hid_r, g_s, g_r, tx, n2s, u2s, r2s, mqkv, prob_t,
           mo_s, mo_r, lb_s, lb_r, gh, mof,
           gs_s, gs_r, dq_s, dq_r,
           fxs, fys, ax, ay, wa, wb, ra1, rb1, sa1, sb1, ra2, rb2, p3, r3, fin, finr,
           gv1, gr1, gv2, gr2, gv3, gr3, gv4, gr4,
           ld, w_ss, w_rs, f_ss, f_rs, q_ss, q_rs, o_ss, o_rs, h_ss, h_rs, g_ss, g_rs,
           m_ss, m_rs, l_ss, l_rs, gs_ss, gs_rs, dq_ss, dq_rs, x_ss, x_rs,
           a1_ss, a1_rs, b1_ss, b1_rs, a2_ss, a2_rs, b2_ss, b2_rs, r3_ss, r3_rs, e_ss, e_rs,
           v_ss, v_rs):
    i, j = lax.axis_index("frame"), lax.axis_index("quad")
    core, z, x_lo = i % 2, (i // 2) % 8, i // 16
    y, x_hi = j % 4, j // 4
    x = x_hi * 2 + x_lo
    sib = (i + 1 - 2 * core, j)

    def fpeer(d):
        return (i + d) % 32

    def qpeer(d):
        return (j + d) % 8

    def xpeer(d):
        xx = (x + d) % 4
        return ((xx % 2) * 16 + i % 16, (xx // 2) * 4 + y)

    def ypeer(d):
        return (i, x_hi * 4 + (y + d) % 4)

    def zpeer(d):
        return (x_lo * 16 + ((z + d) % 8) * 2 + core, j)

    def remote(src, dst, ss, rs, dev):
        return pltpu.make_async_remote_copy(
            src_ref=src, dst_ref=dst, send_sem=ss, recv_sem=rs, device_id=dev, device_id_type=MESH)

    bar = pltpu.get_barrier_semaphore()

    @pl.loop(1, 32)
    def _(d):
        pl.semaphore_signal(bar, inc=1, device_id=(fpeer(d), j), device_id_type=MESH)

    @pl.loop(1, 8)
    def _(d):
        pl.semaphore_signal(bar, inc=1, device_id=(i, qpeer(d)), device_id_type=MESH)

    diag = (((x_lo + 1) % 2) * 16 + i % 16, ((x_hi + 1) % 2) * 4 + y)
    pl.semaphore_signal(bar, inc=1, device_id=diag, device_id_type=MESH)

    loads = [
        pltpu.make_async_copy(act_h, act, ld.at[0]),
        pltpu.make_async_copy(spw_h.at[0], spw.at[0], ld.at[1]),
        pltpu.make_async_copy(spw_h.at[1], spw.at[1], ld.at[2]),
        pltpu.make_async_copy(spw_h.at[2], spw.at[2], ld.at[3]),
        pltpu.make_async_copy(spw_h.at[3], spw.at[3], ld.at[4]),
        pltpu.make_async_copy(cot_h, cot, ld.at[5]),
        pltpu.make_async_copy(mw_h, mw.at[:, j], ld.at[6]),
        pltpu.make_async_copy(pe_h, pe, ld.at[7]),
        pltpu.make_async_copy(perm_h, perm, ld.at[8]),
    ]
    for c in loads:
        c.start()
    pl.semaphore_wait(bar, 39)

    def w_copy(t, d):
        return remote(mw_h.at[2 * core + t], mw.at[2 * core + t, j], w_ss.at[8 * t + d], w_rs.at[8 * t + d], (i, qpeer(d)))

    def w_forward(t, d):
        part = mw.at[2 * core + t, (j - d + 8) % 8]
        return remote(part, part, f_ss.at[8 * t + d], f_rs.at[8 * t + d], sib)

    for t in range(2):
        @pl.loop(1, 8)
        def _(d, t=t):
            w_copy(t, d).start()

    loads[0].wait()
    u1, _ = unit(act[...].astype(F32))
    n1 = (u1 * spg[...]).astype(BF)
    for t in range(3):
        loads[1 + t].wait()
        for hp, part in enumerate(split_pair(nn(n1, spw[t]))):
            qkv_s[hp * 4:hp * 4 + 4, t] = part.astype(BF).reshape(4, 32, 384)

    def q_copy(d):
        return remote(qkv_s.at[qpeer(d)], qkv_r.at[j], q_ss.at[d], q_rs.at[d], (i, qpeer(d)))

    @pl.loop(1, 8)
    def _(d):
        q_copy(d).start()

    qkv_r[j] = qkv_s[j]

    @pl.loop(1, 8)
    def _(d):
        q_copy(d).wait()

    q, k, v = (qkv_r[:, t].reshape(256, 384) for t in range(3))
    out = None
    for h in range(2):
        probs = softmax(head_of(q, h), k)
        prob_s[h] = probs
        term = nn(probs.astype(BF), head_of(v, h))
        out = term if out is None else out + term
    o_s[...] = out.astype(BF).reshape(8, 32, 384)

    def o_copy(d):
        return remote(o_s.at[qpeer(d)], o_r.at[j], o_ss.at[d], o_rs.at[d], (i, qpeer(d)))

    @pl.loop(1, 8)
    def _(d):
        o_copy(d).start()

    o_r[j] = o_s[j]

    loads[5].wait()
    loads[8].wait()

    @pl.loop(1, 8)
    def _(d):
        o_copy(d).wait()

    loads[4].wait()
    so = join_pair(o_r[0:4].reshape(128, 384).astype(F32), o_r[4:8].reshape(128, 384).astype(F32)).astype(BF)
    hid[...] = (act[...].astype(F32) + nt(so, spw[3])).astype(BF)
    scatter_rows(hid_s, nn(row_order(), hid[...]))

    def h_copy(d):
        return remote(hid_s.at[fpeer(d)], hid_r.at[i], h_ss.at[d], h_rs.at[d], (fpeer(d), j))

    @pl.loop(1, 32)
    def _(d):
        h_copy(d).start()

    hid_r[i] = hid_s[i]

    loads[6].wait()
    for t in range(2):
        @pl.loop(1, 8)
        def _(d, t=t):
            w_copy(t, d).wait()
            w_forward(t, d).start()

    for t in range(2):
        @pl.loop(1, 8)
        def _(d, t=t):
            w_forward(t, d).wait()

    def weight(n):
        return mw[n].reshape(C, W)

    grad_out = nn(cot[...], weight(3)).astype(BF)
    scatter_rows(g_s, nn(row_order(), grad_out))

    def g_copy(d):
        return remote(g_s.at[fpeer(d)], g_r.at[i], g_ss.at[d], g_rs.at[d], (fpeer(d), j))

    @pl.loop(1, 32)
    def _(d):
        g_copy(d).start()

    g_r[i] = g_s[i]

    @pl.loop(1, 32)
    def _(d):
        h_copy(d).wait()

    gather_rows(tx, hid_r)
    loads[7].wait()
    u2, r2 = unit(tx[...])
    u2s[...] = u2
    r2s[...] = jnp.broadcast_to(r2, r2s.shape)
    n2s[...] = (u2 * mgn[...] + pe[...]).astype(BF)
    for t in range(3):
        mqkv[t] = nn(n2s[...], weight(t)).astype(BF)
    out = None
    for h in range(HEADS):
        probs = softmax(head_of(mqkv[0], h), mqkv[1])
        prob_t[h] = probs
        term = nn(probs.astype(BF), head_of(mqkv[2], h))
        out = term if out is None else out + term
    scatter_rows(mo_s, out)

    def m_copy(d):
        return remote(mo_s.at[fpeer(d)], mo_r.at[i], m_ss.at[d], m_rs.at[d], (fpeer(d), j))

    @pl.loop(1, 32)
    def _(d):
        m_copy(d).start()

    mo_r[i] = mo_s[i]

    @pl.loop(1, 32)
    def _(d):
        g_copy(d).wait()

    gather_rows(mof, g_r)
    mg = mof[...].astype(BF)
    dq, dk, dv = attend_back(mqkv[0], mqkv[1], mqkv[2], mg, prob_t, HEADS)
    dq, dk, dv = dq.astype(BF), dk.astype(BF), dv.astype(BF)
    dn2 = nt(dq, weight(0)) + nt(dk, weight(1)) + nt(dv, weight(2))
    u2 = u2s[...]
    gv1[...] = jnp.sum(dn2 * u2, axis=0, keepdims=True)
    back = unit_back(dn2, u2, r2s[:, 0:1], mgn[...])
    scatter_rows(lb_s, back)

    def l_copy(d):
        return remote(lb_s.at[fpeer(d)], lb_r.at[i], l_ss.at[d], l_rs.at[d], (fpeer(d), j))

    @pl.loop(1, 32)
    def _(d):
        l_copy(d).start()

    lb_r[i] = lb_s[i]

    @pl.loop(1, 32)
    def _(d):
        m_copy(d).wait()

    gather_rows(mof, mo_r)
    mo = tn(row_order(), mof[...].astype(BF)).astype(BF)

    n2p = nn(n2s[...], perm[...]).astype(BF)
    ctp = nn(cot[...], perm[...]).astype(BF)
    ax[0, 0:128] = n2p
    fxs[0] = n2p

    @pl.when(core == 0)
    def _():
        ax[1, 0:128] = n2p
        ay[0, 0:128] = dq
        ay[1, 0:128] = dk
        fxs[1] = ctp
        fys[0] = dv
        fys[1] = mo

    @pl.when(core == 1)
    def _():
        ax[1, 0:128] = ctp
        ay[0, 0:128] = dv
        ay[1, 0:128] = mo
        fxs[1] = n2p
        fys[0] = dq
        fys[1] = dk

    swap = [remote(fxs, ax.at[:, 128:256], x_ss.at[0], x_rs.at[0], sib),
            remote(fys, ay.at[:, 128:256], x_ss.at[1], x_rs.at[1], sib)]
    for c in swap:
        c.start()
    bo[...] = (hid[...].astype(F32) + nt(mo, weight(3))).astype(BF)
    for c in swap:
        c.wait()

    wa[...] = tn(ax[0], ay[0]).astype(BF)

    def a1_copy(d):
        to = pl.multiple_of(((x + d) % 4) * 320, 16)
        return remote(wa.at[pl.ds(to, 320)], ra1.at[d - 1], a1_ss.at[d], a1_rs.at[d], xpeer(d))

    def v_copy(src, dst, n, dev):
        return remote(src, dst, v_ss.at[n], v_rs.at[n], dev)

    for d in (1, 3, 2):
        a1_copy(d).start()
    gx = [v_copy(gv1, gr1.at[d - 1], d, xpeer(d)) for d in range(1, 4)]
    for c in gx:
        c.start()

    wb[...] = tn(ax[1], ay[1]).astype(BF)

    def b1_copy(d, n):
        to = pl.multiple_of(n * 320 + ((y + d) % 4) * 80, 16)
        return remote(wb.at[pl.ds(to, 80)], rb1.at[d - 1, n], b1_ss.at[d, n], b1_rs.at[d, n], ypeer(d))

    for d in (1, 3, 2):
        for n in range(4):
            b1_copy(d, n).start()

    @pl.loop(1, 32)
    def _(d):
        l_copy(d).wait()

    gather_rows(tx, lb_r)
    gh[...] = (cot[...].astype(F32) + tn(row_order(), tx[...].astype(BF))).astype(BF)
    ghb = gh[...]
    for hp, part in enumerate(split_pair(nn(ghb, spw[3]))):
        gs_s[hp * 4:hp * 4 + 4] = part.astype(BF).reshape(4, 32, 384)

    def gs_copy(d):
        return remote(gs_s.at[qpeer(d)], gs_r.at[j], gs_ss.at[d], gs_rs.at[d], (i, qpeer(d)))

    @pl.loop(1, 8)
    def _(d):
        gs_copy(d).start()

    gs_r[j] = gs_s[j]

    @pl.loop(1, 8)
    def _(d):
        gs_copy(d).wait()

    q, k, v = (qkv_r[:, t].reshape(256, 384) for t in range(3))
    for t, grad in enumerate(attend_back(q, k, v, gs_r[...].reshape(256, 384), prob_s, 2)):
        dq_s[:, t] = grad.astype(BF).reshape(8, 32, 384)

    def dq_copy(d):
        return remote(dq_s.at[qpeer(d)], dq_r.at[j], dq_ss.at[d], dq_rs.at[d], (i, qpeer(d)))

    @pl.loop(1, 8)
    def _(d):
        dq_copy(d).start()

    dq_r[j] = dq_s[j]

    for d in (1, 3, 2):
        a1_copy(d).wait()
    mine = pl.multiple_of(x * 320, 16)
    sa1[...] = (wa[pl.ds(mine, 320), :].astype(F32) + ra1[0].astype(F32) + ra1[1].astype(F32) + ra1[2].astype(F32)).astype(BF)

    def a2_copy(d):
        to = pl.multiple_of(((y + d) % 4) * 80, 16)
        return remote(sa1.at[pl.ds(to, 80)], ra2.at[d - 1], a2_ss.at[d], a2_rs.at[d], ypeer(d))

    for d in range(1, 4):
        a2_copy(d).start()
    for c in gx:
        c.wait()
    gv2[...] = gv1[...] + gr1[0] + gr1[1] + gr1[2]
    gy = [v_copy(gv2, gr2.at[d - 1], 3 + d, ypeer(d)) for d in range(1, 4)]
    for c in gy:
        c.start()

    for d in (1, 3, 2):
        for n in range(4):
            b1_copy(d, n).wait()
    for n in range(4):
        mine = pl.multiple_of(n * 320 + y * 80, 16)
        sb1[n] = (wb[pl.ds(mine, 80), :].astype(F32) + rb1[0, n].astype(F32) + rb1[1, n].astype(F32) + rb1[2, n].astype(F32)).astype(BF)

    def b2_copy(d):
        return remote(sb1.at[(x + d) % 4], rb2.at[d - 1], b2_ss.at[d], b2_rs.at[d], xpeer(d))

    for d in range(1, 4):
        b2_copy(d).start()
    for c in gy:
        c.wait()
    gv3[...] = gv2[...] + gr2[0] + gr2[1] + gr2[2]
    gz = [v_copy(gv3, gr3.at[d - 1], 6 + d, zpeer(d)) for d in range(1, 8)]
    for c in gz:
        c.start()

    @pl.loop(1, 8)
    def _(d):
        dq_copy(d).wait()

    total = None
    for t in range(3):
        grad = join_pair(dq_r[0:4, t].reshape(128, 384).astype(F32), dq_r[4:8, t].reshape(128, 384).astype(F32)).astype(BF)
        term = nt(grad, spw[t])
        total = term if total is None else total + term
    u1, r1 = unit(act[...].astype(F32))
    ig[...] = (gh[...].astype(F32) + unit_back(total, u1, r1, spg[...])).astype(BF)

    for d in range(1, 4):
        a2_copy(d).wait()
    for d in range(1, 4):
        b2_copy(d).wait()
    row = lax.broadcasted_iota(jnp.int32, (128, 80), 0)
    col = lax.broadcasted_iota(jnp.int32, (128, 80), 1)
    place = jnp.where((row % 16 < 10) & (col == (row // 16) * 10 + row % 16), 1.0, 0.0).astype(BF)
    mine = pl.multiple_of(y * 80, 16)
    s2 = sa1[pl.ds(mine, 80), :].astype(F32) + ra2[0].astype(F32) + ra2[1].astype(F32) + ra2[2].astype(F32)
    p3[:, 0:16] = nn(place, s2.astype(BF)).astype(BF).reshape(8, 16, W)
    s2 = sb1[x].astype(F32) + rb2[0].astype(F32) + rb2[1].astype(F32) + rb2[2].astype(F32)
    p3[:, 16:32] = nn(place, s2.astype(BF)).astype(BF).reshape(8, 16, W)

    def z_copy(d):
        return remote(p3.at[(z + d) % 8], r3.at[d - 1], r3_ss.at[d], r3_rs.at[d], zpeer(d))

    for d in range(1, 8):
        z_copy(d).start()
    for c in gz:
        c.wait()
    total = gv3[...]
    for d in range(7):
        total = total + gr3[d]
    gv4[...] = total
    last_v = v_copy(gv4, gr4, 14, sib)
    last_v.start()
    for d in range(1, 8):
        z_copy(d).wait()
    total = p3[z].astype(F32)
    for d in range(7):
        total = total + r3[d].astype(F32)
    fin[...] = total
    last = remote(fin, finr, e_ss.at[0], e_rs.at[0], sib)
    last.start()
    last_v.wait()
    factor = 1.0 / math.sqrt(128 * 256)
    gn[...] = (gv4[...] + gr4[...]) * factor
    last.wait()

    @pl.when(core == 0)
    def _():
        wg[0] = fin[0:5, :] * factor
        wg[1] = fin[16:21, :] * factor
        wg[2] = finr[0:5, :] * factor
        wg[3] = finr[16:21, :] * factor

    @pl.when(core == 1)
    def _():
        wg[0] = finr[5:10, :] * factor
        wg[1] = finr[21:26, :] * factor
        wg[2] = fin[5:10, :] * factor
        wg[3] = fin[21:26, :] * factor


def positional(frames, channels):
    freq = np.exp(np.arange(channels // 2, dtype=np.float32)[None, :] * np.float32(-2.0 * math.log(10000.0) / channels))
    phases = np.arange(frames, dtype=np.float32)[:, None] * freq.astype(np.float32)
    both = np.stack([np.sin(phases.astype(np.float64)), np.cos(phases.astype(np.float64))], axis=-1)
    return both.reshape(frames, channels).astype(np.float32)


def permutation():
    order = np.arange(C).reshape(2, 8, 2, 2, 4, 5)
    order = order.transpose(3, 0, 4, 1, 2, 5).reshape(-1)
    matrix = np.zeros((C, C), np.float32)
    matrix[order, np.arange(C)] = 1.0
    return matrix


def local(activations, cotangent, spatial_weights, spatial_gain, motion_weights, motion_gain):
    pe = jnp.asarray(positional(128, C))
    perm = jnp.asarray(permutation(), dtype=BF)
    V, D = pltpu.VMEM, pltpu.SemaphoreType.DMA
    any_, vmem = pl.BlockSpec(memory_space=pl.ANY), pl.BlockSpec(memory_space=pltpu.VMEM)
    scratch = [
        V((128, C), BF), V((128, C), BF), V((4, C, W), BF), V((4, 8, 160, W), BF), V((128, C), F32), V((C, C), BF),
        V((8, 3, 32, 384), BF), V((8, 3, 32, 384), BF), V((8, 32, 384), BF), V((8, 32, 384), BF), V((2, 256, 256), F32),
        V((128, C), BF), V((32, 4, C), BF), V((32, 4, C), BF), V((32, 4, W), BF), V((32, 4, W), BF),
        V((128, C), F32), V((128, C), BF), V((128, C), F32), V((128, 128), F32), V((3, 128, W), BF), V((4, 128, 128), F32),
        V((32, 4, W), BF), V((32, 4, W), BF), V((32, 4, C), BF), V((32, 4, C), BF), V((128, C), BF), V((128, W), F32),
        V((8, 32, 384), BF), V((8, 32, 384), BF), V((8, 3, 32, 384), BF), V((8, 3, 32, 384), BF),
        V((2, 128, C), BF), V((2, 128, W), BF), V((2, 256, C), BF), V((2, 256, W), BF), V((C, W), BF), V((C, W), BF),
        V((3, 320, W), BF), V((3, 4, 80, W), BF), V((320, W), BF), V((4, 80, W), BF), V((3, 80, W), BF), V((3, 80, W), BF),
        V((8, 32, W), BF), V((7, 32, W), BF), V((32, W), F32), V((32, W), F32),
        V((1, C), F32), V((3, 1, C), F32), V((1, C), F32), V((3, 1, C), F32), V((1, C), F32), V((7, 1, C), F32),
        V((1, C), F32), V((1, C), F32),
        D((9,)), D((16,)), D((16,)), D((16,)), D((16,)), D((8,)), D((8,)), D((8,)), D((8,)),
        D((32,)), D((32,)), D((32,)), D((32,)), D((32,)), D((32,)), D((32,)), D((32,)),
        D((8,)), D((8,)), D((8,)), D((8,)), D((2,)), D((2,)),
        D((4,)), D((4,)), D((4, 4)), D((4, 4)), D((4,)), D((4,)), D((4,)), D((4,)), D((8,)), D((8,)), D((1,)), D((1,)),
        D((16,)), D((16,)),
    ]
    block_output, input_grad, weight_grad, gain_all = pl.pallas_call(
        kernel,
        out_shape=(
            jax.ShapeDtypeStruct((128, C), BF),
            jax.ShapeDtypeStruct((128, C), BF),
            jax.ShapeDtypeStruct((4, 5, W), F32),
            jax.ShapeDtypeStruct((1, C), F32),
        ),
        in_specs=[any_, any_, any_, vmem, any_, vmem, any_, any_],
        out_specs=(vmem, vmem, vmem, vmem),
        scratch_shapes=scratch,
        compiler_params=pltpu.CompilerParams(
            has_side_effects=True, collective_id=0, vmem_limit_bytes=60 * 2 ** 20),
    )(
        activations.reshape(128, C), cotangent.reshape(128, C), spatial_weights, spatial_gain.reshape(1, C),
        motion_weights, motion_gain.reshape(1, C), pe, perm,
    )
    device = lax.axis_index("frame") * 8 + lax.axis_index("quad")
    gain_grad = lax.dynamic_slice_in_dim(gain_all.reshape(C), device * 5, 5)
    shape = activations.shape
    return block_output.reshape(shape), input_grad.reshape(shape), weight_grad, gain_grad


def solution(mesh):
    in_specs = (
        P("frame", "quad", None),
        P("frame", "quad", None),
        P(),
        P(),
        P(None, "quad", None),
        P(),
    )
    out_specs = (
        P("frame", "quad", None),
        P("frame", "quad", None),
        P(None, ("frame", "quad"), None),
        P(("frame", "quad")),
    )
    return jax.shard_map(local, mesh=mesh, in_specs=in_specs, out_specs=out_specs, check_vma=False)
```

time: 763 us -> 163 us (0.21)
  waiting for transfers between devices: 458 us -> 0 us
  Pallas kernels: 0 us -> 153 us
  blocking collectives: 76.5 us -> 0 us
  local copies, waits for them, and re-layouts: 84.7 us -> 8.79 us
  matrix products: 62.7 us -> 0 us
  starting transfers between devices: 34.7 us -> 0 us
  other arithmetic: 24.2 us -> 0 us
  between operations: 14.9 us -> 0.65 us
    unnamed x7 -> x0, waiting for transfers between devices: 290 us -> none
    pallas_call x0 -> x1, Pallas kernels: none -> 153 us  [local(): pl.pallas_call(kernel, out_shape=(jax.ShapeDtypeStruct((128, C), BF), jax...]
    all_gather x3 -> x0, waiting for transfers between devices: 120 us -> none  [the longest x1 52 us: local(): lax.all_gather(spatial_keys, 'quad', axis=1, tiled=True)]
    unnamed x1 -> x0, blocking collectives: 76.5 us -> none
    dot_general x32 -> x0, matrix products: 62.7 us -> none  [the longest x8 17.4 us: project(): result = jnp.dot(flattened, weight, preferred_element_type=jnp.float32)]
    convert_element_type x17 -> x0, local copies, waits for them, and re-layouts: 46.3 us -> none  [the longest x5 34.5 us: local(): cell_wide = by_cell.astype(jnp.float32)]
    all_to_all x4 -> x0, starting transfers between devices: 34.2 us -> none  [the longest x2 20.6 us: to_positions(): lax.all_to_all(values, 'frame', split_axis=1, concat_axis=0, tiled=True)]
    reduce_scatter x2 -> x0, waiting for transfers between devices: 24.8 us -> none  [the longest x1 24.7 us: local(): lax.psum_scatter(value_terms.astype(jnp.bfloat16), 'quad', scatter_dimens...]
  transfers between devices with their start and end apart: 10 -> 0, of which waited for: 7 -> 0; matrix products, arithmetic and copies ran while one was open for 14% -> 0% of each run, Pallas kernels for 0% -> 0%
where the time goes in v1:
time: 163 us; the launch traced here: 162 us
  Pallas kernels  153 us (94%)
  local copies, waits for them, and re-layouts  8.79 us (5%)
    pallas_call x1, Pallas kernels, local(): pl.pallas_call(kernel, out_shape=(jax.ShapeDtypeStruct((128, C), BF), jax...  153 us
    unnamed x3, local copies, waits for them, and re-layouts  4.95 us

profile of v1, /device:TPU:1, one launch (start us, length us, event | category | flops | bytes accessed | tf_op | source)
XLA Modules:
  0.0 162.3 jit_solution(10906170773887922210)
XLA Ops:
  0.6 1.3 reshape.30.spg
  1.9 1.3 reshape.31.mgn
  3.2 152.9 %shard_map.111 = (bf16[128,1280]{1,0:T(8,128)(2,1)}, bf16[128,1280]{1,0:T(8,128)(2,1)}, f32[4,5,640]{2,1,0:T(8,128)}, f32[1,1280]{1,0:T(1,128)}) custom-call(bf16[128,1280]{1,0:T(8,128)(2,1)} %bitcast.6, bf16[128,1280]{1,0:T(8,128)(2,1)} %bitcast.7, bf16[4,1280,640]{2,1,0:T(8,128)(2,1)} %spw_h.1, f32[1,1280]{1,0:T(1,128)} %reshape.30.spg, ...), custom_call_target="tpu_custom_call" | custom-call | tf_op jit(solution)/shard_map/pallas_call | solution.py:554
  156.1 1.3 dynamic-slice_bitcast_fusion
  157.4 1.5 copy.12
  158.9 1.7 %copy.15 = bf16[4,32,1280]{2,1,0:T(8,128)(2,1)} copy(bf16[4,32,1280]{2,1,0:T(8,128)(2,1)} %bitcast.9) | data formatting | bytes 655360
  160.6 1.7 %copy.16 = bf16[4,32,1280]{2,1,0:T(8,128)(2,1)} copy(bf16[4,32,1280]{2,1,0:T(8,128)(2,1)} %bitcast.8) | data formatting | bytes 655360

commit v2 on v1

v2 whole, which is shorter than its diff:
```python
import math

import jax
import jax.numpy as jnp
import numpy as np
from jax import lax
from jax.experimental import pallas as pl
from jax.experimental.pallas import tpu as pltpu
from jax.sharding import PartitionSpec as P

HEADS = 4
HEAD_DIM = 160
EPSILON = 1e-05
SCALE = HEAD_DIM ** (-0.5)
C = 1280
W = 640
F32 = jnp.float32
BF = jnp.bfloat16
MESH = pl.DeviceIdType.MESH


def nn(a, b):
    return jnp.dot(a, b, preferred_element_type=F32)


def nt(a, b):
    return lax.dot_general(a, b, (((1,), (1,)), ((), ())), preferred_element_type=F32)


def tn(a, b):
    return lax.dot_general(a, b, (((0,), (0,)), ((), ())), preferred_element_type=F32)


def unit(x):
    xc = x - jnp.mean(x, axis=-1, keepdims=True)
    r = lax.rsqrt(jnp.mean(xc * xc, axis=-1, keepdims=True) + EPSILON)
    return xc * r, r


def unit_back(grad, u, r, gain):
    g = grad * gain
    return r * (g - jnp.mean(g, axis=-1, keepdims=True) - u * jnp.mean(g * u, axis=-1, keepdims=True))


def head_of(x, h):
    lane = lax.broadcasted_iota(jnp.int32, x.shape, 1)
    return jnp.where((lane >= h * HEAD_DIM) & (lane < (h + 1) * HEAD_DIM), x, jnp.zeros_like(x))


def split_pair(y):
    return y[:, :384], pltpu.roll(y, 320, 1)[:, :384]


def join_pair(a, b):
    pad = jnp.zeros((a.shape[0], 256), F32)
    left = jnp.concatenate([a, pad], axis=1)
    right = pltpu.roll(jnp.concatenate([b, pad], axis=1), 320, 1)
    lane = lax.broadcasted_iota(jnp.int32, left.shape, 1)
    return jnp.where(lane < 320, left, right)


def row_order():
    row = lax.broadcasted_iota(jnp.int32, (128, 128), 0)
    col = lax.broadcasted_iota(jnp.int32, (128, 128), 1)
    return jnp.where(col == (row % 4) * 32 + row // 4, 1.0, 0.0).astype(BF)


def scatter_rows(to, rows):
    for n in range(32):
        to[n] = rows[4 * n:4 * n + 4, :].astype(BF)


def gather_rows(rows, come):
    for n in range(32):
        rows[4 * n:4 * n + 4, :] = come[n].astype(F32)


def softmax(q, k):
    s = nt(q, k) * SCALE
    e = jnp.exp(s - jnp.max(s, axis=-1, keepdims=True))
    return e / jnp.sum(e, axis=-1, keepdims=True)


def attend_back(q, k, v, g, probs, heads):
    dq = dk = dv = None
    for h in range(heads):
        r = probs[h]
        dr = nt(head_of(g, h), v)
        delta = jnp.sum(r * dr, axis=-1, keepdims=True)
        ds = (r * (dr - delta) * SCALE).astype(BF)
        a, b, c = nn(ds, head_of(k, h)), tn(ds, head_of(q, h)), tn(r.astype(BF), head_of(g, h))
        dq, dk, dv = (a, b, c) if dq is None else (dq + a, dk + b, dv + c)
    return dq, dk, dv


def kernel(act_h, cot_h, spw_h, spg, mw_h, mgn, pe_h, perm_h,
           bo_h, ig_h, wg, gn,
           act, cot, spw, mw, pe, perm, bo, ig,
           qkv_s, qkv_r, o_s, o_r, prob_s,
           hid, hid_s, hid_r, ct_s, ct_r, ctt, tx, n2s, u2s, r2s, mqkv, prob_t,
           mo_s, mo_r, lb_s, lb_r, gh, mof,
           gs_s, gs_r, dq_s, dq_r,
           fx, fy, ax, ay, wa, wb, rax, ray, rbx, rby, sax, say, sbx, sby, tax, tay, tbx, tby, p3, r3,
           gv1, gr1, gv2, gr2,
           ld, st, w1_ss, w1_rs, w2_ss, w2_rs, w3_ss, w3_rs, w4_ss, w4_rs,
           q_ss, q_rs, o_ss, o_rs, h_ss, h_rs, c_ss, c_rs,
           m_ss, m_rs, l_ss, l_rs, gs_ss, gs_rs, dq_ss, dq_rs, x_ss, x_rs,
           ax_ss, ax_rs, ay_ss, ay_rs, bx_ss, bx_rs, by_ss, by_rs,
           ax2_ss, ax2_rs, ay2_ss, ay2_rs, bx2_ss, bx2_rs, by2_ss, by2_rs, r3_ss, r3_rs,
           v_ss, v_rs):
    i, j = lax.axis_index("frame"), lax.axis_index("quad")
    core, z, x_lo = i % 2, (i // 2) % 8, i // 16
    y, x_hi = j % 4, j // 4
    x = x_hi * 2 + x_lo
    zc = i % 16
    sib = (i + 1 - 2 * core, j)
    cross = ((1 - x_lo) * 16 + zc, (1 - x_hi) * 4 + y)
    beside = ((1 - x_lo) * 16 + zc, j)

    def fpeer(d):
        return (i + d) % 32

    def qpeer(d):
        return (j + d) % 8

    def xpeer(d):
        xx = (x + d) % 4
        return ((xx % 2) * 16 + zc, (xx // 2) * 4 + y)

    def ypeer(d):
        return (i, x_hi * 4 + (y + d) % 4)

    def remote(src, dst, ss, rs, dev):
        return pltpu.make_async_remote_copy(
            src_ref=src, dst_ref=dst, send_sem=ss, recv_sem=rs, device_id=dev, device_id_type=MESH)

    def arrived(part, ss, rs):
        pltpu.make_async_copy(part, part, ss).wait()
        pltpu.make_async_copy(part, part, rs).wait()

    bar = pltpu.get_barrier_semaphore()

    @pl.loop(1, 32)
    def _(d):
        pl.semaphore_signal(bar, inc=1, device_id=(fpeer(d), j), device_id_type=MESH)

    @pl.loop(1, 8)
    def _(d):
        pl.semaphore_signal(bar, inc=1, device_id=(i, qpeer(d)), device_id_type=MESH)

    pl.semaphore_signal(bar, inc=1, device_id=cross, device_id_type=MESH)

    half = pl.ds(pl.multiple_of(core * 80, 16), 80)
    loads = [
        pltpu.make_async_copy(act_h, act, ld.at[0]),
        pltpu.make_async_copy(spw_h.at[0], spw.at[0], ld.at[1]),
        pltpu.make_async_copy(spw_h.at[1], spw.at[1], ld.at[2]),
        pltpu.make_async_copy(spw_h.at[2], spw.at[2], ld.at[3]),
        pltpu.make_async_copy(cot_h, cot, ld.at[5]),
        pltpu.make_async_copy(mw_h.at[:, half], mw.at[:, j, half], ld.at[6]),
        pltpu.make_async_copy(spw_h.at[3], spw.at[3], ld.at[4]),
        pltpu.make_async_copy(pe_h, pe, ld.at[7]),
        pltpu.make_async_copy(perm_h, perm, ld.at[8]),
    ]
    for c in loads:
        c.start()

    loads[0].wait()
    u1, _ = unit(act[...].astype(F32))
    n1 = (u1 * spg[...].reshape(1, C)).astype(BF)
    for t in range(3):
        loads[1 + t].wait()
        for hp, part in enumerate(split_pair(nn(n1, spw[t]))):
            qkv_s[hp * 4:hp * 4 + 4, t] = part.astype(BF).reshape(4, 32, 384)
    pl.semaphore_wait(bar, 39)

    def q_copy(d):
        return remote(qkv_s.at[qpeer(d)], qkv_r.at[j], q_ss.at[0], q_rs.at[0], (i, qpeer(d)))

    @pl.loop(1, 8)
    def _(d):
        q_copy(d).start()

    def w1_copy(n, d):
        return remote(mw_h.at[n, half], mw.at[n, j, half], w1_ss.at[n], w1_rs.at[n], ypeer(d))

    def w2_copy(n):
        part = mw.at[n, pl.ds(x_hi * 4 + 2 * (1 - x_lo), 2), half]
        return remote(part, part, w2_ss.at[n], w2_rs.at[n], cross)

    def w3_copy(n):
        part = mw.at[n, pl.ds((1 - x_hi) * 4 + 2 * x_lo, 2), half]
        return remote(part, part, w3_ss.at[n], w3_rs.at[n], beside)

    def w4_copy(n):
        part = mw.at[n, :, half]
        return remote(part, part, w4_ss.at[n], w4_rs.at[n], sib)

    def w1_start(n):
        for d in (1, 3, 2):
            w1_copy(n, d).start()

    def w1_pass(n):
        arrived(mw.at[n, 0:3, half], w1_ss.at[n], w1_rs.at[n])
        w2_copy(n).start()

    def w2_pass(n):
        w2_copy(n).wait()
        w3_copy(n).start()

    def w3_pass(n):
        w3_copy(n).wait()
        w4_copy(n).start()

    w1_start(0)
    w1_start(1)

    loads[4].wait()
    scatter_rows(ct_s, nn(row_order(), cot[...]))

    def c_copy(d):
        return remote(ct_s.at[fpeer(d)], ct_r.at[i], c_ss.at[0], c_rs.at[0], (fpeer(d), j))

    @pl.loop(1, 32)
    def _(d):
        c_copy(d).start()

    ct_r[i] = ct_s[i]
    loads[5].wait()
    qkv_r[j] = qkv_s[j]

    arrived(qkv_r.at[0:7], q_ss.at[0], q_rs.at[0])

    q, k, v = (qkv_r[:, t].reshape(256, 384) for t in range(3))
    out = None
    for h in range(2):
        probs = softmax(head_of(q, h), k)
        prob_s[h] = probs
        term = nn(probs.astype(BF), head_of(v, h))
        out = term if out is None else out + term
    o_s[...] = out.astype(BF).reshape(8, 32, 384)

    def o_copy(d):
        return remote(o_s.at[qpeer(d)], o_r.at[j], o_ss.at[0], o_rs.at[0], (i, qpeer(d)))

    @pl.loop(1, 8)
    def _(d):
        o_copy(d).start()

    o_r[j] = o_s[j]
    w1_start(2)
    w1_start(3)
    w1_pass(0)
    w1_pass(1)

    arrived(o_r.at[0:7], o_ss.at[0], o_rs.at[0])

    loads[6].wait()
    so = join_pair(o_r[0:4].reshape(128, 384).astype(F32), o_r[4:8].reshape(128, 384).astype(F32)).astype(BF)
    hid[...] = (act[...].astype(F32) + nt(so, spw[3])).astype(BF)
    scatter_rows(hid_s, nn(row_order(), hid[...]))

    def h_copy(d):
        return remote(hid_s.at[fpeer(d)], hid_r.at[i], h_ss.at[0], h_rs.at[0], (fpeer(d), j))

    @pl.loop(1, 32)
    def _(d):
        h_copy(d).start()

    hid_r[i] = hid_s[i]

    w2_pass(0)

    arrived(ct_r.at[0:31], c_ss.at[0], c_rs.at[0])

    gather_rows(tx, ct_r)
    ctt[...] = tx[...].astype(BF)
    loads[8].wait()
    ctp = nn(ctt[...], perm[...]).astype(BF)

    @pl.when(core == 0)
    def _():
        ax[0, 0:128] = ctp

    @pl.when(core == 1)
    def _():
        fx[0] = ctp

    w2_pass(1)
    w3_pass(0)
    w1_pass(2)
    w3_pass(1)
    w1_pass(3)
    w2_pass(2)
    w3_pass(2)
    w2_pass(3)
    w3_pass(3)

    def weight(n):
        return mw[n].reshape(C, W)

    arrived(hid_r.at[0:31], h_ss.at[0], h_rs.at[0])

    gather_rows(tx, hid_r)
    loads[7].wait()
    gain = mgn[...].reshape(1, C)
    u2, r2 = unit(tx[...])
    u2s[...] = u2
    r2s[...] = jnp.broadcast_to(r2, r2s.shape)
    n2s[...] = (u2 * gain + pe[...]).astype(BF)
    for t in range(3):
        w4_copy(t).wait()
        mqkv[t] = nn(n2s[...], weight(t)).astype(BF)
    out = None
    for h in range(HEADS):
        probs = softmax(head_of(mqkv[0], h), mqkv[1])
        prob_t[h] = probs
        term = nn(probs.astype(BF), head_of(mqkv[2], h))
        out = term if out is None else out + term
    mo_t = out.astype(BF)
    scatter_rows(mo_s, out)

    def m_copy(d):
        return remote(mo_s.at[fpeer(d)], mo_r.at[i], m_ss.at[0], m_rs.at[0], (fpeer(d), j))

    @pl.loop(1, 32)
    def _(d):
        m_copy(d).start()

    mo_r[i] = mo_s[i]

    w4_copy(3).wait()
    mg = nn(ctt[...], weight(3)).astype(BF)
    dv = None
    for h in range(HEADS):
        term = tn(prob_t[h].astype(BF), head_of(mg, h))
        dv = term if dv is None else dv + term
    dv = dv.astype(BF)
    n2p = nn(n2s[...], perm[...]).astype(BF)
    ax[1, 0:128] = n2p
    fx[1] = n2p

    @pl.when(core == 0)
    def _():
        ay[0, 0:128] = mo_t
        fx[0] = n2p
        fy[0] = dv

    @pl.when(core == 1)
    def _():
        ax[0, 0:128] = n2p
        ay[0, 0:128] = dv
        fy[0] = mo_t

    swap = [remote(fx.at[0], ax.at[0, 128:256], x_ss.at[0], x_rs.at[0], sib),
            remote(fy.at[0], ay.at[0, 128:256], x_ss.at[1], x_rs.at[1], sib),
            remote(fx.at[1], ax.at[1, 128:256], x_ss.at[2], x_rs.at[2], sib)]
    for c in swap:
        c.start()

    dq = dk = None
    for h in range(HEADS):
        r = prob_t[h]
        dr = nt(head_of(mg, h), mqkv[2])
        delta = jnp.sum(r * dr, axis=-1, keepdims=True)
        ds = (r * (dr - delta) * SCALE).astype(BF)
        a, b = nn(ds, head_of(mqkv[1], h)), tn(ds, head_of(mqkv[0], h))
        dq, dk = (a, b) if dq is None else (dq + a, dk + b)
    dq, dk = dq.astype(BF), dk.astype(BF)

    @pl.when(core == 0)
    def _():
        ay[1, 0:128] = dq
        fy[1] = dk

    @pl.when(core == 1)
    def _():
        ay[1, 0:128] = dk
        fy[1] = dq

    swap_b = remote(fy.at[1], ay.at[1, 128:256], x_ss.at[3], x_rs.at[3], sib)
    swap_b.start()
    for c in swap:
        c.wait()
    wa[...] = tn(ax[0], ay[0]).astype(BF).reshape(4, 4, 80, W)

    def ax_copy(d):
        return remote(wa.at[(x + d) % 4, :, :, 0:384], rax.at[d - 1], ax_ss.at[0], ax_rs.at[0], xpeer(d))

    def ay_copy(d):
        return remote(wa.at[:, (y + d) % 4, :, 384:640], ray.at[d - 1], ay_ss.at[0], ay_rs.at[0], ypeer(d))

    for d in (1, 3, 2):
        ax_copy(d).start()
        ay_copy(d).start()

    dn2 = nt(dq, weight(0)) + nt(dk, weight(1)) + nt(dv, weight(2))
    u2 = u2s[...]
    gv1[...] = jnp.sum(dn2 * u2, axis=0, keepdims=True)
    back = ctt[...].astype(F32) + unit_back(dn2, u2, r2s[:, 0:1], gain)
    scatter_rows(lb_s, back)

    def l_copy(d):
        return remote(lb_s.at[fpeer(d)], lb_r.at[i], l_ss.at[0], l_rs.at[0], (fpeer(d), j))

    @pl.loop(1, 32)
    def _(d):
        l_copy(d).start()

    lb_r[i] = lb_s[i]

    def v_copy(src, dst, n, dev):
        return remote(src, dst, v_ss.at[n], v_rs.at[n], dev)

    gx = [v_copy(gv1, gr1.at[d - 1], 0, xpeer(d)) for d in range(1, 4)]
    for c in gx:
        c.start()

    swap_b.wait()
    wb[...] = tn(ax[1], ay[1]).astype(BF).reshape(4, 4, 80, W)

    arrived(mo_r.at[0:31], m_ss.at[0], m_rs.at[0])

    gather_rows(mof, mo_r)
    mo = tn(row_order(), mof[...].astype(BF)).astype(BF)
    bo[...] = (hid[...].astype(F32) + nt(mo, weight(3))).astype(BF)
    bo_store = pltpu.make_async_copy(bo, bo_h, st.at[0])
    bo_store.start()

    def bx_copy(d):
        return remote(wb.at[(x + d) % 4, :, :, 0:256], rbx.at[d - 1], bx_ss.at[0], bx_rs.at[0], xpeer(d))

    def by_copy(d):
        return remote(wb.at[:, (y + d) % 4, :, 256:640], rby.at[d - 1], by_ss.at[0], by_rs.at[0], ypeer(d))

    arrived(lb_r.at[0:31], l_ss.at[0], l_rs.at[0])

    gather_rows(tx, lb_r)
    gh[...] = tn(row_order(), tx[...].astype(BF)).astype(BF)
    for hp, part in enumerate(split_pair(nn(gh[...], spw[3]))):
        gs_s[hp * 4:hp * 4 + 4] = part.astype(BF).reshape(4, 32, 384)

    def gs_copy(d):
        return remote(gs_s.at[qpeer(d)], gs_r.at[j], gs_ss.at[0], gs_rs.at[0], (i, qpeer(d)))

    @pl.loop(1, 8)
    def _(d):
        gs_copy(d).start()

    gs_r[j] = gs_s[j]
    for d in (1, 3, 2):
        bx_copy(d).start()
        by_copy(d).start()

    arrived(gs_r.at[0:7], gs_ss.at[0], gs_rs.at[0])

    q, k, v = (qkv_r[:, t].reshape(256, 384) for t in range(3))
    for t, grad in enumerate(attend_back(q, k, v, gs_r[...].reshape(256, 384), prob_s, 2)):
        dq_s[:, t] = grad.astype(BF).reshape(8, 32, 384)

    def dq_copy(d):
        return remote(dq_s.at[qpeer(d)], dq_r.at[j], dq_ss.at[0], dq_rs.at[0], (i, qpeer(d)))

    @pl.loop(1, 8)
    def _(d):
        dq_copy(d).start()

    dq_r[j] = dq_s[j]

    def add4(own, parts):
        return own.astype(F32) + parts[0].astype(F32) + parts[1].astype(F32) + parts[2].astype(F32)

    arrived(rax, ax_ss.at[0], ax_rs.at[0])
    arrived(ray, ay_ss.at[0], ay_rs.at[0])
    sax[...] = add4(wa[x, :, :, 0:384], rax).astype(BF)
    say[...] = add4(wa[:, y, :, 384:640], ray).astype(BF)

    def ax2_copy(d):
        return remote(sax.at[(y + d) % 4], tax.at[d - 1], ax2_ss.at[0], ax2_rs.at[0], ypeer(d))

    def ay2_copy(d):
        return remote(say.at[(x + d) % 4], tay.at[d - 1], ay2_ss.at[0], ay2_rs.at[0], xpeer(d))

    for d in (1, 3, 2):
        ax2_copy(d).start()
        ay2_copy(d).start()
    arrived(gr1, v_ss.at[0], v_rs.at[0])
    gv2[...] = gv1[...] + gr1[0] + gr1[1] + gr1[2]
    gy = [v_copy(gv2, gr2.at[d - 1], 1, ypeer(d)) for d in range(1, 4)]
    for c in gy:
        c.start()

    arrived(rbx, bx_ss.at[0], bx_rs.at[0])
    arrived(rby, by_ss.at[0], by_rs.at[0])
    sbx[...] = add4(wb[x, :, :, 0:256], rbx).astype(BF)
    sby[...] = add4(wb[:, y, :, 256:640], rby).astype(BF)

    def bx2_copy(d):
        return remote(sbx.at[(y + d) % 4], tbx.at[d - 1], bx2_ss.at[0], bx2_rs.at[0], ypeer(d))

    def by2_copy(d):
        return remote(sby.at[(x + d) % 4], tby.at[d - 1], by2_ss.at[0], by2_rs.at[0], xpeer(d))

    for d in (1, 3, 2):
        bx2_copy(d).start()
        by2_copy(d).start()

    arrived(dq_r.at[0:7], dq_ss.at[0], dq_rs.at[0])

    total = None
    for t in range(3):
        grad = join_pair(dq_r[0:4, t].reshape(128, 384).astype(F32), dq_r[4:8, t].reshape(128, 384).astype(F32)).astype(BF)
        term = nt(grad, spw[t])
        total = term if total is None else total + term
    u1, r1 = unit(act[...].astype(F32))
    ig[...] = (gh[...].astype(F32) + unit_back(total, u1, r1, spg[...].reshape(1, C))).astype(BF)
    ig_store = pltpu.make_async_copy(ig, ig_h, st.at[1])
    ig_store.start()

    row = lax.broadcasted_iota(jnp.int32, (256, 80), 0)
    col = lax.broadcasted_iota(jnp.int32, (256, 80), 1)
    first = jnp.where((row % 16 < 5) & (col == (row // 16) * 5 + row % 16), 1.0, 0.0).astype(BF)
    second = jnp.where((row % 16 >= 5) & (row % 16 < 10) & (col == (row // 16) * 5 + row % 16 - 5), 1.0, 0.0).astype(BF)
    arrived(gr2, v_ss.at[1], v_rs.at[1])
    gv = gv2[...] + gr2[0] + gr2[1] + gr2[2]
    arrived(tax, ax2_ss.at[0], ax2_rs.at[0])
    arrived(tay, ay2_ss.at[0], ay2_rs.at[0])
    sum_a = jnp.concatenate([add4(sax[y], tax), add4(say[x], tay)], axis=1).astype(BF)
    arrived(tbx, bx2_ss.at[0], bx2_rs.at[0])
    arrived(tby, by2_ss.at[0], by2_rs.at[0])
    sum_b = jnp.concatenate([add4(sbx[y], tbx), add4(sby[x], tby)], axis=1).astype(BF)
    slabs = nn(first, sum_a) + nn(second, sum_b)
    row = lax.broadcasted_iota(jnp.int32, (256, W), 0) % 16
    slabs = jnp.where(row == 10, gv[:, :W], jnp.where(row == 11, gv[:, W:], slabs))
    p3[...] = slabs.astype(BF).reshape(16, 16, W)

    def z_copy(d):
        to = (zc + d) % 16
        return remote(p3.at[to], r3.at[zc], r3_ss.at[0], r3_rs.at[0], (x_lo * 16 + to, j))

    @pl.loop(1, 16)
    def _(d):
        z_copy(d).start()

    r3[zc] = p3[zc]

    arrived(r3.at[0:15], r3_ss.at[0], r3_rs.at[0])

    factor = 1.0 / math.sqrt(128 * 256)
    sums = []
    for c in range(2):
        total = r3[c].astype(F32)
        for n in range(1, 8):
            total = total + r3[2 * n + c].astype(F32)
        sums.append(total * factor)
    wg[:, 0] = sums[0][5:10]
    wg[:, 1] = sums[1][5:10]
    wg[:, 2] = sums[1][0:5]
    wg[:, 3] = sums[0][0:5]
    both = sums[0] + sums[1]
    gn[...] = jnp.concatenate([both[10:11], both[11:12]], axis=1)
    bo_store.wait()
    ig_store.wait()


def finish(bo_h, ig_h, wg_h, gn, bo, ig, wg, gg, bo_v, ig_v, wg_v, sems):
    moves = [(bo_h, bo_v, bo), (ig_h, ig_v, ig), (wg_h, wg_v, wg)]
    come = [pltpu.make_async_copy(a, b, sems.at[0, n]) for n, (a, b, _) in enumerate(moves)]
    go = [pltpu.make_async_copy(b, c, sems.at[1, n]) for n, (_, b, c) in enumerate(moves)]
    for c in come:
        c.start()
    device = lax.axis_index("frame") * 8 + lax.axis_index("quad")
    gg[...] = pltpu.roll(gn[...], C - device * 5, 1)[0, :5]
    for a, b in zip(come, go):
        a.wait()
        b.start()
    for c in go:
        c.wait()


def positional(frames, channels):
    freq = np.exp(np.arange(channels // 2, dtype=np.float32)[None, :] * np.float32(-2.0 * math.log(10000.0) / channels))
    phases = np.arange(frames, dtype=np.float32)[:, None] * freq.astype(np.float32)
    both = np.stack([np.sin(phases.astype(np.float64)), np.cos(phases.astype(np.float64))], axis=-1)
    return both.reshape(frames, channels).astype(np.float32)


def permutation():
    order = np.arange(C).reshape(2, 8, 2, 2, 4, 5)
    order = order.transpose(3, 0, 4, 1, 2, 5).reshape(-1)
    matrix = np.zeros((C, C), np.float32)
    matrix[order, np.arange(C)] = 1.0
    return matrix


def local(activations, cotangent, spatial_weights, spatial_gain, motion_weights, motion_gain):
    pe = jnp.asarray(positional(128, C))
    perm = jnp.asarray(permutation(), dtype=BF)
    V, D = pltpu.VMEM, pltpu.SemaphoreType.DMA
    any_, vmem = pl.BlockSpec(memory_space=pl.ANY), pl.BlockSpec(memory_space=pltpu.VMEM)
    scratch = [
        V((128, C), BF), V((128, C), BF), V((4, C, W), BF), V((4, 8, 160, W), BF), V((128, C), F32), V((C, C), BF),
        V((128, C), BF), V((128, C), BF),
        V((8, 3, 32, 384), BF), V((8, 3, 32, 384), BF), V((8, 32, 384), BF), V((8, 32, 384), BF), V((2, 256, 256), F32),
        V((128, C), BF), V((32, 4, C), BF), V((32, 4, C), BF), V((32, 4, C), BF), V((32, 4, C), BF), V((128, C), BF),
        V((128, C), F32), V((128, C), BF), V((128, C), F32), V((128, 128), F32), V((3, 128, W), BF), V((4, 128, 128), F32),
        V((32, 4, W), BF), V((32, 4, W), BF), V((32, 4, C), BF), V((32, 4, C), BF), V((128, C), BF), V((128, W), F32),
        V((8, 32, 384), BF), V((8, 32, 384), BF), V((8, 3, 32, 384), BF), V((8, 3, 32, 384), BF),
        V((2, 128, C), BF), V((2, 128, W), BF), V((2, 256, C), BF), V((2, 256, W), BF),
        V((4, 4, 80, W), BF), V((4, 4, 80, W), BF),
        V((3, 4, 80, 384), BF), V((3, 4, 80, 256), BF), V((3, 4, 80, 256), BF), V((3, 4, 80, 384), BF),
        V((4, 80, 384), BF), V((4, 80, 256), BF), V((4, 80, 256), BF), V((4, 80, 384), BF),
        V((3, 80, 384), BF), V((3, 80, 256), BF), V((3, 80, 256), BF), V((3, 80, 384), BF),
        V((16, 16, W), BF), V((16, 16, W), BF),
        V((1, C), F32), V((3, 1, C), F32), V((1, C), F32), V((3, 1, C), F32),
        D((9,)), D((2,))] + [D((4,))] * 8 + [D((1,))] * 16 + [D((4,)), D((4,))] + [D((1,))] * 18 + [
        D((2,)), D((2,)),
    ]
    results = (
        jax.ShapeDtypeStruct((128, C), BF),
        jax.ShapeDtypeStruct((128, C), BF),
        jax.ShapeDtypeStruct((5, 4, W), F32),
    )
    block_output, input_grad, weight_grad, gain_all = pl.pallas_call(
        kernel,
        out_shape=results + (jax.ShapeDtypeStruct((1, C), F32),),
        in_specs=[any_, any_, any_, vmem, any_, vmem, any_, any_],
        out_specs=(any_, any_, vmem, vmem),
        scratch_shapes=scratch,
        compiler_params=pltpu.CompilerParams(
            has_side_effects=True, collective_id=0, vmem_limit_bytes=60 * 2 ** 20),
    )(
        activations.reshape(128, C), cotangent.reshape(128, C), spatial_weights, spatial_gain,
        motion_weights, motion_gain, pe, perm,
    )
    block_output, input_grad, weight_grad, gain_grad = pl.pallas_call(
        finish,
        out_shape=results + (jax.ShapeDtypeStruct((5,), F32),),
        in_specs=[any_, any_, any_, vmem],
        out_specs=(any_, any_, any_, vmem),
        scratch_shapes=[V((128, C), BF), V((128, C), BF), V((5, 4, W), F32), D((2, 3))],
        compiler_params=pltpu.CompilerParams(vmem_limit_bytes=60 * 2 ** 20),
    )(block_output, input_grad, weight_grad, gain_all)
    shape = activations.shape
    return block_output.reshape(shape), input_grad.reshape(shape), weight_grad.transpose(1, 0, 2), gain_grad


def solution(mesh):
    in_specs = (
        P("frame", "quad", None),
        P("frame", "quad", None),
        P(),
        P(),
        P(None, "quad", None),
        P(),
    )
    out_specs = (
        P("frame", "quad", None),
        P("frame", "quad", None),
        P(None, ("frame", "quad"), None),
        P(("frame", "quad")),
    )
    return jax.shard_map(local, mesh=mesh, in_specs=in_specs, out_specs=out_specs, check_vma=False)
```

time: 163 us -> 128 us (0.79)
  Pallas kernels: 153 us -> 127 us
  local copies, waits for them, and re-layouts: 8.79 us -> 0 us
    pallas_call x1 -> x2, Pallas kernels: 153 us -> 127 us  [the longest x1 124 us: local(): pl.pallas_call(kernel, out_shape=results + (jax.ShapeDtypeStruct((1, C),...]
    unnamed x3 -> x0, local copies, waits for them, and re-layouts: 4.95 us -> none
    reshape x2 -> x0, local copies, waits for them, and re-layouts: 2.59 us -> none  [the longest x1 1.29 us: local(): spatial_gain.reshape(1, C)]
where the time goes in v2:
time: 128 us; the launch traced here: 127 us
  Pallas kernels  127 us (99%)
    pallas_call x1, Pallas kernels, local(): pl.pallas_call(kernel, out_shape=results + (jax.ShapeDtypeStruct((1, C),...  124 us
    pallas_call x1, Pallas kernels, local(): pl.pallas_call(finish, out_shape=results + (jax.ShapeDtypeStruct((5,), F3...  3.06 us

profile of v2, /device:TPU:1, one launch (start us, length us, event | category | flops | bytes accessed | tf_op | source)
XLA Modules:
  0.0 127.5 jit_solution(10360356728074873266)
XLA Ops:
  0.6 123.6 %shard_map.111 = (bf16[128,1280]{1,0:T(8,128)(2,1)}, bf16[128,1280]{1,0:T(8,128)(2,1)}, f32[5,4,640]{2,1,0:T(4,128)}, f32[1,1280]{1,0:T(1,128)}) custom-call(bf16[128,1280]{1,0:T(8,128)(2,1)} %bitcast.5, bf16[128,1280]{1,0:T(8,128)(2,1)} %bitcast.6, bf16[4,1280,640]{2,1,0:T(8,128)(2,1)} %spw_h.1, f32[1280]{0:T(1024)} %spg.1, bf16[4,160,640]{2,1,0:T(8,128)(2,1)} %mw_h.1, ...), custom_call_target="tpu_custom_call" | custom-call | tf_op jit(solution)/shard_map/pallas_call | solution.py:624
  124.3 3.1 %shard_map.112 = (bf16[128,1280]{1,0:T(8,128)(2,1)}, bf16[128,1280]{1,0:T(8,128)(2,1)}, f32[5,4,640]{2,1,0:T(4,128)}, f32[5]{0:T(128)}) custom-call(bf16[128,1280]{1,0:T(8,128)(2,1)} %get-tuple-element.12.bo_h, bf16[128,1280]{1,0:T(8,128)(2,1)} %get-tuple-element.13.ig_h, f32[5,4,640]{2,1,0:T(4,128)} %get-tuple-element.14.wg_h, f32[1,1280]{1,0:T(1,128)} %get-tuple-element.15.gn), custom_call_target="tpu_custom_call" | custom-call | tf_op jit(solution)/shard_map/pallas_call | solution.py:636

commit v3 on v2

--- a/solution.py
+++ b/solution.py
@@ -252,6 +252,7 @@
     w1_start(3)
     w1_pass(0)
     w1_pass(1)
+    w2_pass(0)
 
     arrived(o_r.at[0:7], o_ss.at[0], o_rs.at[0])
 
@@ -269,8 +270,6 @@
 
     hid_r[i] = hid_s[i]
 
-    w2_pass(0)
-
     arrived(ct_r.at[0:31], c_ss.at[0], c_rs.at[0])
 
     gather_rows(tx, ct_r)
@@ -287,14 +286,13 @@
         fx[0] = ctp
 
     w2_pass(1)
+    w1_pass(2)
     w3_pass(0)
-    w1_pass(2)
+    w1_pass(3)
     w3_pass(1)
-    w1_pass(3)
     w2_pass(2)
+    w2_pass(3)
     w3_pass(2)
-    w2_pass(3)
-    w3_pass(3)
 
     def weight(n):
         return mw[n].reshape(C, W)
@@ -329,6 +327,7 @@
 
     mo_r[i] = mo_s[i]
 
+    w3_pass(3)
     w4_copy(3).wait()
     mg = nn(ctt[...], weight(3)).astype(BF)
     dv = None
@@ -391,7 +390,6 @@
         return remote(wa.at[:, (y + d) % 4, :, 384:640], ray.at[d - 1], ay_ss.at[0], ay_rs.at[0], ypeer(d))
 
     for d in (1, 3, 2):
-        ax_copy(d).start()
         ay_copy(d).start()
 
     dn2 = nt(dq, weight(0)) + nt(dk, weight(1)) + nt(dv, weight(2))
@@ -412,12 +410,24 @@
     def v_copy(src, dst, n, dev):
         return remote(src, dst, v_ss.at[n], v_rs.at[n], dev)
 
+    for d in (1, 3, 2):
+        ax_copy(d).start()
     gx = [v_copy(gv1, gr1.at[d - 1], 0, xpeer(d)) for d in range(1, 4)]
     for c in gx:
         c.start()
 
     swap_b.wait()
     wb[...] = tn(ax[1], ay[1]).astype(BF).reshape(4, 4, 80, W)
+
+    def bx_copy(d):
+        return remote(wb.at[(x + d) % 4, :, :, 0:256], rbx.at[d - 1], bx_ss.at[0], bx_rs.at[0], xpeer(d))
+
+    def by_copy(d):
+        return remote(wb.at[:, (y + d) % 4, :, 256:640], rby.at[d - 1], by_ss.at[0], by_rs.at[0], ypeer(d))
+
+    for d in (1, 3, 2):
+        bx_copy(d).start()
+        by_copy(d).start()
 
     arrived(mo_r.at[0:31], m_ss.at[0], m_rs.at[0])
 
@@ -427,12 +437,6 @@
     bo_store = pltpu.make_async_copy(bo, bo_h, st.at[0])
     bo_store.start()
 
-    def bx_copy(d):
-        return remote(wb.at[(x + d) % 4, :, :, 0:256], rbx.at[d - 1], bx_ss.at[0], bx_rs.at[0], xpeer(d))
-
-    def by_copy(d):
-        return remote(wb.at[:, (y + d) % 4, :, 256:640], rby.at[d - 1], by_ss.at[0], by_rs.at[0], ypeer(d))
-
     arrived(lb_r.at[0:31], l_ss.at[0], l_rs.at[0])
 
     gather_rows(tx, lb_r)
@@ -448,24 +452,6 @@
         gs_copy(d).start()
 
     gs_r[j] = gs_s[j]
-    for d in (1, 3, 2):
-        bx_copy(d).start()
-        by_copy(d).start()
-
-    arrived(gs_r.at[0:7], gs_ss.at[0], gs_rs.at[0])
-
-    q, k, v = (qkv_r[:, t].reshape(256, 384) for t in range(3))
-    for t, grad in enumerate(attend_back(q, k, v, gs_r[...].reshape(256, 384), prob_s, 2)):
-        dq_s[:, t] = grad.astype(BF).reshape(8, 32, 384)
-
-    def dq_copy(d):
-        return remote(dq_s.at[qpeer(d)], dq_r.at[j], dq_ss.at[0], dq_rs.at[0], (i, qpeer(d)))
-
-    @pl.loop(1, 8)
-    def _(d):
-        dq_copy(d).start()
-
-    dq_r[j] = dq_s[j]
 
     def add4(own, parts):
         return own.astype(F32) + parts[0].astype(F32) + parts[1].astype(F32) + parts[2].astype(F32)
@@ -505,17 +491,20 @@
         bx2_copy(d).start()
         by2_copy(d).start()
 
-    arrived(dq_r.at[0:7], dq_ss.at[0], dq_rs.at[0])
-
-    total = None
-    for t in range(3):
-        grad = join_pair(dq_r[0:4, t].reshape(128, 384).astype(F32), dq_r[4:8, t].reshape(128, 384).astype(F32)).astype(BF)
-        term = nt(grad, spw[t])
-        total = term if total is None else total + term
-    u1, r1 = unit(act[...].astype(F32))
-    ig[...] = (gh[...].astype(F32) + unit_back(total, u1, r1, spg[...].reshape(1, C))).astype(BF)
-    ig_store = pltpu.make_async_copy(ig, ig_h, st.at[1])
-    ig_store.start()
+    arrived(gs_r.at[0:7], gs_ss.at[0], gs_rs.at[0])
+
+    q, k, v = (qkv_r[:, t].reshape(256, 384) for t in range(3))
+    for t, grad in enumerate(attend_back(q, k, v, gs_r[...].reshape(256, 384), prob_s, 2)):
+        dq_s[:, t] = grad.astype(BF).reshape(8, 32, 384)
+
+    def dq_copy(d):
+        return remote(dq_s.at[qpeer(d)], dq_r.at[j], dq_ss.at[0], dq_rs.at[0], (i, qpeer(d)))
+
+    @pl.loop(1, 8)
+    def _(d):
+        dq_copy(d).start()
+
+    dq_r[j] = dq_s[j]
 
     row = lax.broadcasted_iota(jnp.int32, (256, 80), 0)
     col = lax.broadcasted_iota(jnp.int32, (256, 80), 1)
@@ -543,6 +532,18 @@
         z_copy(d).start()
 
     r3[zc] = p3[zc]
+
+    arrived(dq_r.at[0:7], dq_ss.at[0], dq_rs.at[0])
+
+    total = None
+    for t in range(3):
+        grad = join_pair(dq_r[0:4, t].reshape(128, 384).astype(F32), dq_r[4:8, t].reshape(128, 384).astype(F32)).astype(BF)
+        term = nt(grad, spw[t])
+        total = term if total is None else total + term
+    u1, r1 = unit(act[...].astype(F32))
+    ig[...] = (gh[...].astype(F32) + unit_back(total, u1, r1, spg[...].reshape(1, C))).astype(BF)
+    ig_store = pltpu.make_async_copy(ig, ig_h, st.at[1])
+    ig_store.start()
 
     arrived(r3.at[0:15], r3_ss.at[0], r3_rs.at[0])
 

time: 128 us -> 111 us (0.87)
  Pallas kernels: 127 us -> 110 us
    pallas_call x1, Pallas kernels: 124 us -> 107 us  [local(): pl.pallas_call(kernel, out_shape=results + (jax.ShapeDtypeStruct((1, C),...]
where the time goes in v3:
time: 111 us
  Pallas kernels  110 us (99%)
    pallas_call x1, Pallas kernels, local(): pl.pallas_call(kernel, out_shape=results + (jax.ShapeDtypeStruct((1, C),...  107 us
    pallas_call x1, Pallas kernels, local(): pl.pallas_call(finish, out_shape=results + (jax.ShapeDtypeStruct((5,), F3...  3.06 us

profile of v3, /device:TPU:1, one launch (start us, length us, event | category | flops | bytes accessed | tf_op | source)
XLA Modules:
  0.0 110.8 jit_solution(3335128291386251736)
XLA Ops:
  0.6 106.9 %shard_map.111 = (bf16[128,1280]{1,0:T(8,128)(2,1)}, bf16[128,1280]{1,0:T(8,128)(2,1)}, f32[5,4,640]{2,1,0:T(4,128)}, f32[1,1280]{1,0:T(1,128)}) custom-call(bf16[128,1280]{1,0:T(8,128)(2,1)} %bitcast.5, bf16[128,1280]{1,0:T(8,128)(2,1)} %bitcast.6, bf16[4,1280,640]{2,1,0:T(8,128)(2,1)} %spw_h.1, f32[1280]{0:T(1024)} %spg.1, bf16[4,160,640]{2,1,0:T(8,128)(2,1)} %mw_h.1, ...), custom_call_target="tpu_custom_call" | custom-call | tf_op jit(solution)/shard_map/pallas_call | solution.py:625
  107.6 3.1 %shard_map.112 = (bf16[128,1280]{1,0:T(8,128)(2,1)}, bf16[128,1280]{1,0:T(8,128)(2,1)}, f32[5,4,640]{2,1,0:T(4,128)}, f32[5]{0:T(128)}) custom-call(bf16[128,1280]{1,0:T(8,128)(2,1)} %get-tuple-element.12.bo_h, bf16[128,1280]{1,0:T(8,128)(2,1)} %get-tuple-element.13.ig_h, f32[5,4,640]{2,1,0:T(4,128)} %get-tuple-element.14.wg_h, f32[1,1280]{1,0:T(1,128)} %get-tuple-element.15.gn), custom_call_target="tpu_custom_call" | custom-call | tf_op jit(solution)/shard_map/pallas_call | solution.py:637

commit v4 on v3

--- a/solution.py
+++ b/solution.py
@@ -16,6 +16,16 @@
 W = 640
 F32 = jnp.float32
 BF = jnp.bfloat16
+XA, XB, YA, YB, ZA, ZB = range(6)
+DIGIT = {XB: 0, XA: 1, YB: 2, YA: 3, ZA: 4, ZB: 4}
+PARTS = (
+    (0, 0, 256, (XB, ZA)),
+    (0, 256, 256, (YA, ZB)),
+    (0, 512, 128, (YB, ZA)),
+    (1, 0, 256, (XA, ZB)),
+    (1, 256, 256, (YB, ZA)),
+    (1, 512, 128, (XB, ZB)),
+)
 MESH = pl.DeviceIdType.MESH
 
 
@@ -100,14 +110,13 @@
            hid, hid_s, hid_r, ct_s, ct_r, ctt, tx, n2s, u2s, r2s, mqkv, prob_t,
            mo_s, mo_r, lb_s, lb_r, gh, mof,
            gs_s, gs_r, dq_s, dq_r,
-           fx, fy, ax, ay, wa, wb, rax, ray, rbx, rby, sax, say, sbx, sby, tax, tay, tbx, tby, p3, r3,
-           gv1, gr1, gv2, gr2,
-           ld, st, w1_ss, w1_rs, w2_ss, w2_rs, w3_ss, w3_rs, w4_ss, w4_rs,
+           fx, fy, ax, ay, wa, wb, p3, r3,
+           gv1, gr1, gv2, gr2, gv3, gr3,
+           ld, st, w1_ss, w1_rs, w2_ss, w2_rs, w3_ss, w3_rs, w4_ss, w4_rs, wz_ss, wz_rs,
            q_ss, q_rs, o_ss, o_rs, h_ss, h_rs, c_ss, c_rs,
            m_ss, m_rs, l_ss, l_rs, gs_ss, gs_rs, dq_ss, dq_rs, x_ss, x_rs,
-           ax_ss, ax_rs, ay_ss, ay_rs, bx_ss, bx_rs, by_ss, by_rs,
-           ax2_ss, ax2_rs, ay2_ss, ay2_rs, bx2_ss, bx2_rs, by2_ss, by2_rs, r3_ss, r3_rs,
-           v_ss, v_rs):
+           p_ss, p_rs, r3_ss, r3_rs,
+           v_ss, v_rs, *buffers):
     i, j = lax.axis_index("frame"), lax.axis_index("quad")
     core, z, x_lo = i % 2, (i // 2) % 8, i // 16
     y, x_hi = j % 4, j // 4
@@ -116,6 +125,9 @@
     sib = (i + 1 - 2 * core, j)
     cross = ((1 - x_lo) * 16 + zc, (1 - x_hi) * 4 + y)
     beside = ((1 - x_lo) * 16 + zc, j)
+    even = z % 2
+    above = (x_lo * 16 + (zc + 2) % 16, j)
+    below = (x_lo * 16 + (zc + 14) % 16, j)
 
     def fpeer(d):
         return (i + d) % 32
@@ -148,7 +160,9 @@
     def _(d):
         pl.semaphore_signal(bar, inc=1, device_id=(i, qpeer(d)), device_id_type=MESH)
 
-    pl.semaphore_signal(bar, inc=1, device_id=cross, device_id_type=MESH)
+    @pl.loop(1, 8)
+    def _(d):
+        pl.semaphore_signal(bar, inc=1, device_id=((1 - x_lo) * 16 + zc, qpeer(d)), device_id_type=MESH)
 
     half = pl.ds(pl.multiple_of(core * 80, 16), 80)
     loads = [
@@ -157,7 +171,8 @@
         pltpu.make_async_copy(spw_h.at[1], spw.at[1], ld.at[2]),
         pltpu.make_async_copy(spw_h.at[2], spw.at[2], ld.at[3]),
         pltpu.make_async_copy(cot_h, cot, ld.at[5]),
-        pltpu.make_async_copy(mw_h.at[:, half], mw.at[:, j, half], ld.at[6]),
+        pltpu.make_async_copy(mw_h.at[even, half], mw.at[even, j, half], ld.at[6]),
+        pltpu.make_async_copy(mw_h.at[2:4, half], mw.at[2:4, j, half], ld.at[9]),
         pltpu.make_async_copy(spw_h.at[3], spw.at[3], ld.at[4]),
         pltpu.make_async_copy(pe_h, pe, ld.at[7]),
         pltpu.make_async_copy(perm_h, perm, ld.at[8]),
@@ -172,7 +187,7 @@
         loads[1 + t].wait()
         for hp, part in enumerate(split_pair(nn(n1, spw[t]))):
             qkv_s[hp * 4:hp * 4 + 4, t] = part.astype(BF).reshape(4, 32, 384)
-    pl.semaphore_wait(bar, 39)
+    pl.semaphore_wait(bar, 45)
 
     def q_copy(d):
         return remote(qkv_s.at[qpeer(d)], qkv_r.at[j], q_ss.at[0], q_rs.at[0], (i, qpeer(d)))
@@ -181,27 +196,37 @@
     def _(d):
         q_copy(d).start()
 
+    matrix = (even, 1 - even, 2, 3)
+
     def w1_copy(n, d):
-        return remote(mw_h.at[n, half], mw.at[n, j, half], w1_ss.at[n], w1_rs.at[n], ypeer(d))
+        m = matrix[n]
+        return remote(mw_h.at[m, half], mw.at[m, j, half], w1_ss.at[n], w1_rs.at[n], ypeer(d))
 
     def w2_copy(n):
-        part = mw.at[n, pl.ds(x_hi * 4 + 2 * (1 - x_lo), 2), half]
+        part = mw.at[matrix[n], pl.ds(x_hi * 4 + 2 * (1 - x_lo), 2), half]
         return remote(part, part, w2_ss.at[n], w2_rs.at[n], cross)
 
     def w3_copy(n):
-        part = mw.at[n, pl.ds((1 - x_hi) * 4 + 2 * x_lo, 2), half]
+        part = mw.at[matrix[n], pl.ds((1 - x_hi) * 4 + 2 * x_lo, 2), half]
         return remote(part, part, w3_ss.at[n], w3_rs.at[n], beside)
 
     def w4_copy(n):
-        part = mw.at[n, :, half]
+        part = mw.at[matrix[n], :, half]
         return remote(part, part, w4_ss.at[n], w4_rs.at[n], sib)
+
+    def wz_copies(group, n):
+        up, down = mw.at[even, pl.ds(group * 4, 2), half], mw.at[even, pl.ds(group * 4 + 2, 2), half]
+        return [remote(up, up, wz_ss.at[n], wz_rs.at[n], above),
+                remote(down, down, wz_ss.at[n + 1], wz_rs.at[n + 1], below)]
+
+    wz = wz_copies(x_hi, 0) + wz_copies(1 - x_hi, 2)
 
     def w1_start(n):
         for d in (1, 3, 2):
             w1_copy(n, d).start()
 
     def w1_pass(n):
-        arrived(mw.at[n, 0:3, half], w1_ss.at[n], w1_rs.at[n])
+        arrived(mw.at[matrix[n], 0:3, half], w1_ss.at[n], w1_rs.at[n])
         w2_copy(n).start()
 
     def w2_pass(n):
@@ -213,7 +238,6 @@
         w4_copy(n).start()
 
     w1_start(0)
-    w1_start(1)
 
     loads[4].wait()
     scatter_rows(ct_s, nn(row_order(), cot[...]))
@@ -227,6 +251,7 @@
 
     ct_r[i] = ct_s[i]
     loads[5].wait()
+    loads[6].wait()
     qkv_r[j] = qkv_s[j]
 
     arrived(qkv_r.at[0:7], q_ss.at[0], q_rs.at[0])
@@ -251,12 +276,13 @@
     w1_start(2)
     w1_start(3)
     w1_pass(0)
-    w1_pass(1)
+    wz[0].start()
+    wz[1].start()
     w2_pass(0)
 
     arrived(o_r.at[0:7], o_ss.at[0], o_rs.at[0])
 
-    loads[6].wait()
+    loads[7].wait()
     so = join_pair(o_r[0:4].reshape(128, 384).astype(F32), o_r[4:8].reshape(128, 384).astype(F32)).astype(BF)
     hid[...] = (act[...].astype(F32) + nt(so, spw[3])).astype(BF)
     scatter_rows(hid_s, nn(row_order(), hid[...]))
@@ -270,11 +296,16 @@
 
     hid_r[i] = hid_s[i]
 
+    w1_pass(2)
+    w3_pass(0)
+    wz[2].start()
+    wz[3].start()
+
     arrived(ct_r.at[0:31], c_ss.at[0], c_rs.at[0])
 
     gather_rows(tx, ct_r)
     ctt[...] = tx[...].astype(BF)
-    loads[8].wait()
+    loads[9].wait()
     ctp = nn(ctt[...], perm[...]).astype(BF)
 
     @pl.when(core == 0)
@@ -285,12 +316,11 @@
     def _():
         fx[0] = ctp
 
-    w2_pass(1)
-    w1_pass(2)
-    w3_pass(0)
     w1_pass(3)
-    w3_pass(1)
     w2_pass(2)
+    for c in wz:
+        c.wait()
+    w4_copy(1).start()
     w2_pass(3)
     w3_pass(2)
 
@@ -300,15 +330,19 @@
     arrived(hid_r.at[0:31], h_ss.at[0], h_rs.at[0])
 
     gather_rows(tx, hid_r)
-    loads[7].wait()
+    loads[8].wait()
     gain = mgn[...].reshape(1, C)
     u2, r2 = unit(tx[...])
     u2s[...] = u2
     r2s[...] = jnp.broadcast_to(r2, r2s.shape)
     n2s[...] = (u2 * gain + pe[...]).astype(BF)
+    w4_copy(0).wait()
+    w4_copy(1).wait()
     for t in range(3):
-        w4_copy(t).wait()
+        if t == 2:
+            w4_copy(2).wait()
         mqkv[t] = nn(n2s[...], weight(t)).astype(BF)
+    w3_pass(3)
     out = None
     for h in range(HEADS):
         probs = softmax(head_of(mqkv[0], h), mqkv[1])
@@ -327,7 +361,6 @@
 
     mo_r[i] = mo_s[i]
 
-    w3_pass(3)
     w4_copy(3).wait()
     mg = nn(ctt[...], weight(3)).astype(BF)
     dv = None
@@ -381,17 +414,72 @@
     swap_b.start()
     for c in swap:
         c.wait()
-    wa[...] = tn(ax[0], ay[0]).astype(BF).reshape(4, 4, 80, W)
-
-    def ax_copy(d):
-        return remote(wa.at[(x + d) % 4, :, :, 0:384], rax.at[d - 1], ax_ss.at[0], ax_rs.at[0], xpeer(d))
-
-    def ay_copy(d):
-        return remote(wa.at[:, (y + d) % 4, :, 384:640], ray.at[d - 1], ay_ss.at[0], ay_rs.at[0], ypeer(d))
-
-    for d in (1, 3, 2):
-        ay_copy(d).start()
-
+    wa[...] = tn(ax[0], ay[0]).reshape(2, 2, 2, 2, 2, 40, W).astype(BF)
+
+    own = (x_hi, (x_hi + x_lo) % 2, y // 2, (y // 2 + y) % 2, z % 2)
+
+    def zpeer(zz):
+        return (x_lo * 16 + (zz + 8) % 8 * 2 + core, j)
+
+    partner = {
+        XA: beside, XB: cross,
+        YA: (i, x_hi * 4 + y + 1 - 2 * (y % 2)), YB: (i, x_hi * 4 + 3 - y),
+        ZA: zpeer(z + 1 - 2 * (z % 2)), ZB: zpeer(z - 1 + 2 * (z % 2)),
+    }
+
+    def left(p, step):
+        return [n for n in range(5) if n not in [DIGIT[link] for link in PARTS[p][3][:step]]]
+
+    def block(p, step, digits):
+        which, lane, lanes, _ = PARTS[p]
+        ref, columns = ((wa, wb)[which], slice(lane, lane + lanes)) if step == 0 else (buffers[6 * p + 2 * step - 1], slice(None))
+        return ref, tuple(digits.get(n, slice(None)) for n in left(p, step)) + (slice(None), columns)
+
+    def step_copy(p, step):
+        link = PARTS[p][3][step]
+        ref, at = block(p, step, {DIGIT[link]: 1 - own[DIGIT[link]]})
+        return remote(ref.at[at], buffers[6 * p + 2 * step], p_ss.at[3 * p + step], p_rs.at[3 * p + step], partner[link])
+
+    def direct(p):
+        digits = left(p, 2)
+        for mask in range(1, 8):
+            to = [own[n] for n in range(4)]
+            for bit, n in enumerate(digits):
+                if mask >> bit & 1:
+                    to[n] = 1 - own[n]
+            ref, at = block(p, 2, {n: to[n] for n in digits})
+            device = ((to[0] + to[1]) % 2 * 16 + zc, to[0] * 4 + to[2] * 2 + (to[2] + to[3]) % 2)
+            remote(ref.at[at], buffers[6 * p + 4].at[mask - 1], p_ss.at[3 * p + 2], p_rs.at[3 * p + 2], device).start()
+
+    done = [0] * 6
+
+    def begin(p):
+        step_copy(p, 0).start()
+
+    def advance(p):
+        step = done[p]
+        step_copy(p, step).wait()
+        link = PARTS[p][3][step]
+        ref, at = block(p, step, {DIGIT[link]: own[DIGIT[link]]})
+        buffers[6 * p + 2 * step + 1][...] = (
+            ref[at].astype(F32) + buffers[6 * p + 2 * step][...].astype(F32)).astype(BF)
+        done[p] = step + 1
+        if step == 0:
+            step_copy(p, 1).start()
+        else:
+            direct(p)
+
+    def result(p):
+        come = buffers[6 * p + 4]
+        arrived(come, p_ss.at[3 * p + 2], p_rs.at[3 * p + 2])
+        ref, at = block(p, 2, {n: own[n] for n in left(p, 2)})
+        total = ref[at].astype(F32)
+        for n in range(7):
+            total = total + come[n].astype(F32)
+        return total.astype(BF)
+
+    for p in (0, 1, 2):
+        begin(p)
     dn2 = nt(dq, weight(0)) + nt(dk, weight(1)) + nt(dv, weight(2))
     u2 = u2s[...]
     gv1[...] = jnp.sum(dn2 * u2, axis=0, keepdims=True)
@@ -410,24 +498,15 @@
     def v_copy(src, dst, n, dev):
         return remote(src, dst, v_ss.at[n], v_rs.at[n], dev)
 
-    for d in (1, 3, 2):
-        ax_copy(d).start()
     gx = [v_copy(gv1, gr1.at[d - 1], 0, xpeer(d)) for d in range(1, 4)]
     for c in gx:
         c.start()
 
     swap_b.wait()
-    wb[...] = tn(ax[1], ay[1]).astype(BF).reshape(4, 4, 80, W)
-
-    def bx_copy(d):
-        return remote(wb.at[(x + d) % 4, :, :, 0:256], rbx.at[d - 1], bx_ss.at[0], bx_rs.at[0], xpeer(d))
-
-    def by_copy(d):
-        return remote(wb.at[:, (y + d) % 4, :, 256:640], rby.at[d - 1], by_ss.at[0], by_rs.at[0], ypeer(d))
-
-    for d in (1, 3, 2):
-        bx_copy(d).start()
-        by_copy(d).start()
+    wb[...] = tn(ax[1], ay[1]).reshape(2, 2, 2, 2, 2, 40, W).astype(BF)
+
+    for p in (3, 4, 5):
+        begin(p)
 
     arrived(mo_r.at[0:31], m_ss.at[0], m_rs.at[0])
 
@@ -437,6 +516,10 @@
     bo_store = pltpu.make_async_copy(bo, bo_h, st.at[0])
     bo_store.start()
 
+    advance(2)
+    advance(0)
+    advance(1)
+
     arrived(lb_r.at[0:31], l_ss.at[0], l_rs.at[0])
 
     gather_rows(tx, lb_r)
@@ -453,45 +536,21 @@
 
     gs_r[j] = gs_s[j]
 
-    def add4(own, parts):
-        return own.astype(F32) + parts[0].astype(F32) + parts[1].astype(F32) + parts[2].astype(F32)
-
-    arrived(rax, ax_ss.at[0], ax_rs.at[0])
-    arrived(ray, ay_ss.at[0], ay_rs.at[0])
-    sax[...] = add4(wa[x, :, :, 0:384], rax).astype(BF)
-    say[...] = add4(wa[:, y, :, 384:640], ray).astype(BF)
-
-    def ax2_copy(d):
-        return remote(sax.at[(y + d) % 4], tax.at[d - 1], ax2_ss.at[0], ax2_rs.at[0], ypeer(d))
-
-    def ay2_copy(d):
-        return remote(say.at[(x + d) % 4], tay.at[d - 1], ay2_ss.at[0], ay2_rs.at[0], xpeer(d))
-
-    for d in (1, 3, 2):
-        ax2_copy(d).start()
-        ay2_copy(d).start()
     arrived(gr1, v_ss.at[0], v_rs.at[0])
     gv2[...] = gv1[...] + gr1[0] + gr1[1] + gr1[2]
     gy = [v_copy(gv2, gr2.at[d - 1], 1, ypeer(d)) for d in range(1, 4)]
     for c in gy:
         c.start()
-
-    arrived(rbx, bx_ss.at[0], bx_rs.at[0])
-    arrived(rby, by_ss.at[0], by_rs.at[0])
-    sbx[...] = add4(wb[x, :, :, 0:256], rbx).astype(BF)
-    sby[...] = add4(wb[:, y, :, 256:640], rby).astype(BF)
-
-    def bx2_copy(d):
-        return remote(sbx.at[(y + d) % 4], tbx.at[d - 1], bx2_ss.at[0], bx2_rs.at[0], ypeer(d))
-
-    def by2_copy(d):
-        return remote(sby.at[(x + d) % 4], tby.at[d - 1], by2_ss.at[0], by2_rs.at[0], xpeer(d))
-
-    for d in (1, 3, 2):
-        bx2_copy(d).start()
-        by2_copy(d).start()
-
+    advance(4)
+    advance(5)
+    advance(3)
     arrived(gs_r.at[0:7], gs_ss.at[0], gs_rs.at[0])
+    advance(2)
+    advance(0)
+    advance(1)
+    advance(4)
+    advance(5)
+    advance(3)
 
     q, k, v = (qkv_r[:, t].reshape(256, 384) for t in range(3))
     for t, grad in enumerate(attend_back(q, k, v, gs_r[...].reshape(256, 384), prob_s, 2)):
@@ -506,32 +565,35 @@
 
     dq_r[j] = dq_s[j]
 
-    row = lax.broadcasted_iota(jnp.int32, (256, 80), 0)
-    col = lax.broadcasted_iota(jnp.int32, (256, 80), 1)
+    arrived(gr2, v_ss.at[1], v_rs.at[1])
+    gv3[...] = gv2[...] + gr2[0] + gr2[1] + gr2[2]
+    gz = v_copy(gv3, gr3, 2, partner[ZA])
+    gz.start()
+
+    row = lax.broadcasted_iota(jnp.int32, (128, 40), 0)
+    col = lax.broadcasted_iota(jnp.int32, (128, 40), 1)
     first = jnp.where((row % 16 < 5) & (col == (row // 16) * 5 + row % 16), 1.0, 0.0).astype(BF)
     second = jnp.where((row % 16 >= 5) & (row % 16 < 10) & (col == (row // 16) * 5 + row % 16 - 5), 1.0, 0.0).astype(BF)
-    arrived(gr2, v_ss.at[1], v_rs.at[1])
-    gv = gv2[...] + gr2[0] + gr2[1] + gr2[2]
-    arrived(tax, ax2_ss.at[0], ax2_rs.at[0])
-    arrived(tay, ay2_ss.at[0], ay2_rs.at[0])
-    sum_a = jnp.concatenate([add4(sax[y], tax), add4(say[x], tay)], axis=1).astype(BF)
-    arrived(tbx, bx2_ss.at[0], bx2_rs.at[0])
-    arrived(tby, by2_ss.at[0], by2_rs.at[0])
-    sum_b = jnp.concatenate([add4(sbx[y], tbx), add4(sby[x], tby)], axis=1).astype(BF)
+    gz.wait()
+    gv = gv3[...] + gr3[...]
+    sum_a = jnp.concatenate([result(p) for p in (0, 1, 2)], axis=1)
+    sum_b = jnp.concatenate([result(p) for p in (3, 4, 5)], axis=1)
     slabs = nn(first, sum_a) + nn(second, sum_b)
-    row = lax.broadcasted_iota(jnp.int32, (256, W), 0) % 16
+    row = lax.broadcasted_iota(jnp.int32, (128, W), 0) % 16
     slabs = jnp.where(row == 10, gv[:, :W], jnp.where(row == 11, gv[:, W:], slabs))
-    p3[...] = slabs.astype(BF).reshape(16, 16, W)
+    p3[...] = slabs.astype(BF).reshape(8, 16, W)
+    place = z // 2 * 2 + core
 
     def z_copy(d):
-        to = (zc + d) % 16
-        return remote(p3.at[to], r3.at[zc], r3_ss.at[0], r3_rs.at[0], (x_lo * 16 + to, j))
-
-    @pl.loop(1, 16)
+        to = (place + d) % 8
+        return remote(p3.at[to], r3.at[place], r3_ss.at[0], r3_rs.at[0],
+                      (x_lo * 16 + to // 2 * 4 + z % 2 * 2 + to % 2, j))
+
+    @pl.loop(1, 8)
     def _(d):
         z_copy(d).start()
 
-    r3[zc] = p3[zc]
+    r3[place] = p3[place]
 
     arrived(dq_r.at[0:7], dq_ss.at[0], dq_rs.at[0])
 
@@ -545,13 +607,13 @@
     ig_store = pltpu.make_async_copy(ig, ig_h, st.at[1])
     ig_store.start()
 
-    arrived(r3.at[0:15], r3_ss.at[0], r3_rs.at[0])
+    arrived(r3.at[0:7], r3_ss.at[0], r3_rs.at[0])
 
     factor = 1.0 / math.sqrt(128 * 256)
     sums = []
     for c in range(2):
         total = r3[c].astype(F32)
-        for n in range(1, 8):
+        for n in range(1, 4):
             total = total + r3[2 * n + c].astype(F32)
         sums.append(total * factor)
     wg[:, 0] = sums[0][5:10]
@@ -587,11 +649,24 @@
 
 
 def permutation():
-    order = np.arange(C).reshape(2, 8, 2, 2, 4, 5)
-    order = order.transpose(3, 0, 4, 1, 2, 5).reshape(-1)
     matrix = np.zeros((C, C), np.float32)
-    matrix[order, np.arange(C)] = 1.0
+    for m in range(C):
+        rest, r = divmod(m, 5)
+        rest, core = divmod(rest, 2)
+        rest, z_high = divmod(rest, 4)
+        xb, xa, yb, ya, z_low = (rest // 16) % 2, (rest // 8) % 2, (rest // 4) % 2, (rest // 2) % 2, rest % 2
+        y = yb * 2 + (yb + ya) % 2
+        n = (xb + xa) % 2 * 640 + (z_high * 2 + z_low) * 80 + core * 40 + xb * 20 + y * 5 + r
+        matrix[n, m] = 1.0
     return matrix
+
+
+def part_buffers():
+    shapes = []
+    for _, _, lanes, _ in PARTS:
+        shapes += [pltpu.VMEM((2, 2, 2, 2, 40, lanes), BF)] * 2 + [pltpu.VMEM((2, 2, 2, 40, lanes), BF)] * 2
+        shapes += [pltpu.VMEM((7, 40, lanes), BF), pltpu.VMEM((8, 128), BF)]
+    return shapes
 
 
 def local(activations, cotangent, spatial_weights, spatial_gain, motion_weights, motion_gain):
@@ -608,15 +683,12 @@
         V((32, 4, W), BF), V((32, 4, W), BF), V((32, 4, C), BF), V((32, 4, C), BF), V((128, C), BF), V((128, W), F32),
         V((8, 32, 384), BF), V((8, 32, 384), BF), V((8, 3, 32, 384), BF), V((8, 3, 32, 384), BF),
         V((2, 128, C), BF), V((2, 128, W), BF), V((2, 256, C), BF), V((2, 256, W), BF),
-        V((4, 4, 80, W), BF), V((4, 4, 80, W), BF),
-        V((3, 4, 80, 384), BF), V((3, 4, 80, 256), BF), V((3, 4, 80, 256), BF), V((3, 4, 80, 384), BF),
-        V((4, 80, 384), BF), V((4, 80, 256), BF), V((4, 80, 256), BF), V((4, 80, 384), BF),
-        V((3, 80, 384), BF), V((3, 80, 256), BF), V((3, 80, 256), BF), V((3, 80, 384), BF),
-        V((16, 16, W), BF), V((16, 16, W), BF),
-        V((1, C), F32), V((3, 1, C), F32), V((1, C), F32), V((3, 1, C), F32),
-        D((9,)), D((2,))] + [D((4,))] * 8 + [D((1,))] * 16 + [D((4,)), D((4,))] + [D((1,))] * 18 + [
-        D((2,)), D((2,)),
-    ]
+        V((2, 2, 2, 2, 2, 40, W), BF), V((2, 2, 2, 2, 2, 40, W), BF), V((8, 16, W), BF), V((8, 16, W), BF),
+        V((1, C), F32), V((3, 1, C), F32), V((1, C), F32), V((3, 1, C), F32), V((1, C), F32), V((1, C), F32),
+        D((10,)), D((2,))] + [D((4,))] * 10 + [D((1,))] * 16 + [
+        D((4,)), D((4,)), D((18,)), D((18,)), D((1,)), D((1,)),
+        D((3,)), D((3,)),
+    ] + part_buffers()
     results = (
         jax.ShapeDtypeStruct((128, C), BF),
         jax.ShapeDtypeStruct((128, C), BF),

time: 111 us -> 106 us (0.955)
  the two profiles are of different devices: /device:TPU:1 before, /device:TPU:25 now
where the time goes in v4:
time: 106 us
  Pallas kernels  105 us (99%)
    pallas_call x1, Pallas kernels, local(): pl.pallas_call(kernel, out_shape=results + (jax.ShapeDtypeStruct((1, C),...  102 us
    pallas_call x1, Pallas kernels, local(): pl.pallas_call(finish, out_shape=results + (jax.ShapeDtypeStruct((5,), F3...  3.06 us

profile of v4, /device:TPU:25, one launch (start us, length us, event | category | flops | bytes accessed | tf_op | source)
XLA Modules:
  0.0 105.7 jit_solution(11308943017620689873)
XLA Ops:
  0.6 101.8 %shard_map.111 = (bf16[128,1280]{1,0:T(8,128)(2,1)}, bf16[128,1280]{1,0:T(8,128)(2,1)}, f32[5,4,640]{2,1,0:T(4,128)}, f32[1,1280]{1,0:T(1,128)}) custom-call(bf16[128,1280]{1,0:T(8,128)(2,1)} %bitcast.5, bf16[128,1280]{1,0:T(8,128)(2,1)} %bitcast.6, bf16[4,1280,640]{2,1,0:T(8,128)(2,1)} %spw_h.1, f32[1280]{0:T(1024)} %spg.1, bf16[4,160,640]{2,1,0:T(8,128)(2,1)} %mw_h.1, ...), custom_call_target="tpu_custom_call" | custom-call | tf_op jit(solution)/shard_map/pallas_call | solution.py:697
  102.4 3.1 %shard_map.112 = (bf16[128,1280]{1,0:T(8,128)(2,1)}, bf16[128,1280]{1,0:T(8,128)(2,1)}, f32[5,4,640]{2,1,0:T(4,128)}, f32[5]{0:T(128)}) custom-call(bf16[128,1280]{1,0:T(8,128)(2,1)} %get-tuple-element.12.bo_h, bf16[128,1280]{1,0:T(8,128)(2,1)} %get-tuple-element.13.ig_h, f32[5,4,640]{2,1,0:T(4,128)} %get-tuple-element.14.wg_h, f32[1,1280]{1,0:T(1,128)} %get-tuple-element.15.gn), custom_call_target="tpu_custom_call" | custom-call | tf_op jit(solution)/shard_map/pallas_call | solution.py:709

commit v5 on v4

--- a/solution.py
+++ b/solution.py
@@ -105,14 +105,14 @@
 
 def kernel(act_h, cot_h, spw_h, spg, mw_h, mgn, pe_h, perm_h,
            bo_h, ig_h, wg, gn,
-           act, cot, spw, mw, pe, perm, bo, ig,
+           act, cot, spw, spt, mw, pe, perm, bo, ig,
            qkv_s, qkv_r, o_s, o_r, prob_s,
            hid, hid_s, hid_r, ct_s, ct_r, ctt, tx, n2s, u2s, r2s, mqkv, prob_t,
            mo_s, mo_r, lb_s, lb_r, gh, mof,
            gs_s, gs_r, dq_s, dq_r,
            fx, fy, ax, ay, wa, wb, p3, r3,
            gv1, gr1, gv2, gr2, gv3, gr3,
-           ld, st, w1_ss, w1_rs, w2_ss, w2_rs, w3_ss, w3_rs, w4_ss, w4_rs, wz_ss, wz_rs,
+           ld, st, w1_ss, w1_rs, w2_ss, w2_rs, w3_ss, w3_rs, w4_ss, w4_rs, wz_ss, wz_rs, wx_ss, wx_rs, wy_ss, wy_rs,
            q_ss, q_rs, o_ss, o_rs, h_ss, h_rs, c_ss, c_rs,
            m_ss, m_rs, l_ss, l_rs, gs_ss, gs_rs, dq_ss, dq_rs, x_ss, x_rs,
            p_ss, p_rs, r3_ss, r3_rs,
@@ -150,20 +150,6 @@
         pltpu.make_async_copy(part, part, ss).wait()
         pltpu.make_async_copy(part, part, rs).wait()
 
-    bar = pltpu.get_barrier_semaphore()
-
-    @pl.loop(1, 32)
-    def _(d):
-        pl.semaphore_signal(bar, inc=1, device_id=(fpeer(d), j), device_id_type=MESH)
-
-    @pl.loop(1, 8)
-    def _(d):
-        pl.semaphore_signal(bar, inc=1, device_id=(i, qpeer(d)), device_id_type=MESH)
-
-    @pl.loop(1, 8)
-    def _(d):
-        pl.semaphore_signal(bar, inc=1, device_id=((1 - x_lo) * 16 + zc, qpeer(d)), device_id_type=MESH)
-
     half = pl.ds(pl.multiple_of(core * 80, 16), 80)
     loads = [
         pltpu.make_async_copy(act_h, act, ld.at[0]),
@@ -180,6 +166,20 @@
     for c in loads:
         c.start()
 
+    bar = pltpu.get_barrier_semaphore()
+
+    @pl.loop(1, 32)
+    def _(d):
+        pl.semaphore_signal(bar, inc=1, device_id=(fpeer(d), j), device_id_type=MESH)
+
+    @pl.loop(1, 8)
+    def _(d):
+        pl.semaphore_signal(bar, inc=1, device_id=(i, qpeer(d)), device_id_type=MESH)
+
+    @pl.loop(1, 8)
+    def _(d):
+        pl.semaphore_signal(bar, inc=1, device_id=((1 - x_lo) * 16 + zc, qpeer(d)), device_id_type=MESH)
+
     loads[0].wait()
     u1, _ = unit(act[...].astype(F32))
     n1 = (u1 * spg[...].reshape(1, C)).astype(BF)
@@ -214,20 +214,33 @@
         part = mw.at[matrix[n], :, half]
         return remote(part, part, w4_ss.at[n], w4_rs.at[n], sib)
 
-    def wz_copies(group, n):
-        up, down = mw.at[even, pl.ds(group * 4, 2), half], mw.at[even, pl.ds(group * 4 + 2, 2), half]
-        return [remote(up, up, wz_ss.at[n], wz_rs.at[n], above),
-                remote(down, down, wz_ss.at[n + 1], wz_rs.at[n + 1], below)]
-
-    wz = wz_copies(x_hi, 0) + wz_copies(1 - x_hi, 2)
+    up, down = mw.at[even, pl.ds(x_hi * 4, 2), half], mw.at[even, pl.ds(x_hi * 4 + 2, 2), half]
+    wz = [remote(up, up, wz_ss.at[0], wz_rs.at[0], above),
+          remote(down, down, wz_ss.at[1], wz_rs.at[1], below)]
+
+    def wx_copy(n):
+        m = matrix[n]
+        return remote(mw_h.at[m, half], mw.at[m, j, half], wx_ss.at[n], wx_rs.at[n], cross)
+
+    def wy_copy(n, d):
+        part = mw.at[matrix[n], (1 - x_hi) * 4 + y, half]
+        return remote(part, part, wy_ss.at[n], wy_rs.at[n], ypeer(d))
 
     def w1_start(n):
         for d in (1, 3, 2):
             w1_copy(n, d).start()
 
-    def w1_pass(n):
+    def w1_wait(n):
         arrived(mw.at[matrix[n], 0:3, half], w1_ss.at[n], w1_rs.at[n])
-        w2_copy(n).start()
+
+    def wy_start(n):
+        wx_copy(n).wait()
+        for d in (1, 3, 2):
+            wy_copy(n, d).start()
+
+    def wy_pass(n):
+        arrived(mw.at[matrix[n], 0:3, half], wy_ss.at[n], wy_rs.at[n])
+        w4_copy(n).start()
 
     def w2_pass(n):
         w2_copy(n).wait()
@@ -237,6 +250,8 @@
         w3_copy(n).wait()
         w4_copy(n).start()
 
+    wx_copy(1).start()
+    wx_copy(3).start()
     w1_start(0)
 
     loads[4].wait()
@@ -253,6 +268,10 @@
     loads[5].wait()
     loads[6].wait()
     qkv_r[j] = qkv_s[j]
+
+    loads[7].wait()
+    for t in range(4):
+        spt[t] = spw[t].T
 
     arrived(qkv_r.at[0:7], q_ss.at[0], q_rs.at[0])
 
@@ -274,17 +293,19 @@
 
     o_r[j] = o_s[j]
     w1_start(2)
+    w1_wait(0)
+    w2_copy(0).start()
+    for c in wz:
+        c.start()
+    wy_start(1)
     w1_start(3)
-    w1_pass(0)
-    wz[0].start()
-    wz[1].start()
     w2_pass(0)
 
     arrived(o_r.at[0:7], o_ss.at[0], o_rs.at[0])
 
-    loads[7].wait()
+    wy_start(3)
     so = join_pair(o_r[0:4].reshape(128, 384).astype(F32), o_r[4:8].reshape(128, 384).astype(F32)).astype(BF)
-    hid[...] = (act[...].astype(F32) + nt(so, spw[3])).astype(BF)
+    hid[...] = (act[...].astype(F32) + nn(so, spt[3])).astype(BF)
     scatter_rows(hid_s, nn(row_order(), hid[...]))
 
     def h_copy(d):
@@ -295,11 +316,8 @@
         h_copy(d).start()
 
     hid_r[i] = hid_s[i]
-
-    w1_pass(2)
-    w3_pass(0)
-    wz[2].start()
-    wz[3].start()
+    w1_wait(2)
+    w2_copy(2).start()
 
     arrived(ct_r.at[0:31], c_ss.at[0], c_rs.at[0])
 
@@ -316,13 +334,11 @@
     def _():
         fx[0] = ctp
 
-    w1_pass(3)
-    w2_pass(2)
     for c in wz:
         c.wait()
-    w4_copy(1).start()
-    w2_pass(3)
-    w3_pass(2)
+    w3_pass(0)
+    wy_pass(1)
+    w2_pass(2)
 
     def weight(n):
         return mw[n].reshape(C, W)
@@ -336,31 +352,25 @@
     u2s[...] = u2
     r2s[...] = jnp.broadcast_to(r2, r2s.shape)
     n2s[...] = (u2 * gain + pe[...]).astype(BF)
+    n2p = nn(n2s[...], perm[...]).astype(BF)
+    ax[1, 0:128] = n2p
+    fx[1] = n2p
+    w3_pass(2)
     w4_copy(0).wait()
     w4_copy(1).wait()
-    for t in range(3):
-        if t == 2:
-            w4_copy(2).wait()
+    for t in range(2):
         mqkv[t] = nn(n2s[...], weight(t)).astype(BF)
-    w3_pass(3)
+    w1_wait(3)
+    wy_pass(3)
+    for h in range(HEADS):
+        prob_t[h] = softmax(head_of(mqkv[0], h), mqkv[1])
+    w4_copy(2).wait()
+    mqkv[2] = nn(n2s[...], weight(2)).astype(BF)
     out = None
     for h in range(HEADS):
-        probs = softmax(head_of(mqkv[0], h), mqkv[1])
-        prob_t[h] = probs
-        term = nn(probs.astype(BF), head_of(mqkv[2], h))
+        term = nn(prob_t[h].astype(BF), head_of(mqkv[2], h))
         out = term if out is None else out + term
     mo_t = out.astype(BF)
-    scatter_rows(mo_s, out)
-
-    def m_copy(d):
-        return remote(mo_s.at[fpeer(d)], mo_r.at[i], m_ss.at[0], m_rs.at[0], (fpeer(d), j))
-
-    @pl.loop(1, 32)
-    def _(d):
-        m_copy(d).start()
-
-    mo_r[i] = mo_s[i]
-
     w4_copy(3).wait()
     mg = nn(ctt[...], weight(3)).astype(BF)
     dv = None
@@ -368,9 +378,6 @@
         term = tn(prob_t[h].astype(BF), head_of(mg, h))
         dv = term if dv is None else dv + term
     dv = dv.astype(BF)
-    n2p = nn(n2s[...], perm[...]).astype(BF)
-    ax[1, 0:128] = n2p
-    fx[1] = n2p
 
     @pl.when(core == 0)
     def _():
@@ -389,6 +396,17 @@
             remote(fx.at[1], ax.at[1, 128:256], x_ss.at[2], x_rs.at[2], sib)]
     for c in swap:
         c.start()
+
+    scatter_rows(mo_s, mo_t.astype(F32))
+
+    def m_copy(d):
+        return remote(mo_s.at[fpeer(d)], mo_r.at[i], m_ss.at[0], m_rs.at[0], (fpeer(d), j))
+
+    @pl.loop(1, 32)
+    def _(d):
+        m_copy(d).start()
+
+    mo_r[i] = mo_s[i]
 
     dq = dk = None
     for h in range(HEADS):
@@ -600,7 +618,7 @@
     total = None
     for t in range(3):
         grad = join_pair(dq_r[0:4, t].reshape(128, 384).astype(F32), dq_r[4:8, t].reshape(128, 384).astype(F32)).astype(BF)
-        term = nt(grad, spw[t])
+        term = nn(grad, spt[t])
         total = term if total is None else total + term
     u1, r1 = unit(act[...].astype(F32))
     ig[...] = (gh[...].astype(F32) + unit_back(total, u1, r1, spg[...].reshape(1, C))).astype(BF)
@@ -675,7 +693,7 @@
     V, D = pltpu.VMEM, pltpu.SemaphoreType.DMA
     any_, vmem = pl.BlockSpec(memory_space=pl.ANY), pl.BlockSpec(memory_space=pltpu.VMEM)
     scratch = [
-        V((128, C), BF), V((128, C), BF), V((4, C, W), BF), V((4, 8, 160, W), BF), V((128, C), F32), V((C, C), BF),
+        V((128, C), BF), V((128, C), BF), V((4, C, W), BF), V((4, W, C), BF), V((4, 8, 160, W), BF), V((128, C), F32), V((C, C), BF),
         V((128, C), BF), V((128, C), BF),
         V((8, 3, 32, 384), BF), V((8, 3, 32, 384), BF), V((8, 32, 384), BF), V((8, 32, 384), BF), V((2, 256, 256), F32),
         V((128, C), BF), V((32, 4, C), BF), V((32, 4, C), BF), V((32, 4, C), BF), V((32, 4, C), BF), V((128, C), BF),
@@ -685,7 +703,7 @@
         V((2, 128, C), BF), V((2, 128, W), BF), V((2, 256, C), BF), V((2, 256, W), BF),
         V((2, 2, 2, 2, 2, 40, W), BF), V((2, 2, 2, 2, 2, 40, W), BF), V((8, 16, W), BF), V((8, 16, W), BF),
         V((1, C), F32), V((3, 1, C), F32), V((1, C), F32), V((3, 1, C), F32), V((1, C), F32), V((1, C), F32),
-        D((10,)), D((2,))] + [D((4,))] * 10 + [D((1,))] * 16 + [
+        D((10,)), D((2,))] + [D((4,))] * 14 + [D((1,))] * 16 + [
         D((4,)), D((4,)), D((18,)), D((18,)), D((1,)), D((1,)),
         D((3,)), D((3,)),
     ] + part_buffers()

time: 106 us -> 97.7 us (0.922)
  the two profiles are of different devices: /device:TPU:25 before, /device:TPU:1 now
where the time goes in v5:
time: 97.7 us; the launch traced here: 96.8 us
  Pallas kernels  96 us (98%)
    pallas_call x1, Pallas kernels, local(): pl.pallas_call(kernel, out_shape=results + (jax.ShapeDtypeStruct((1, C),...  93 us
    pallas_call x1, Pallas kernels, local(): pl.pallas_call(finish, out_shape=results + (jax.ShapeDtypeStruct((5,), F3...  3.06 us

profile of v5, /device:TPU:1, one launch (start us, length us, event | category | flops | bytes accessed | tf_op | source)
XLA Modules:
  0.0 96.8 jit_solution(4037080918386865699)
XLA Ops:
  0.6 93.0 %shard_map.111 = (bf16[128,1280]{1,0:T(8,128)(2,1)}, bf16[128,1280]{1,0:T(8,128)(2,1)}, f32[5,4,640]{2,1,0:T(4,128)}, f32[1,1280]{1,0:T(1,128)}) custom-call(bf16[128,1280]{1,0:T(8,128)(2,1)} %bitcast.5, bf16[128,1280]{1,0:T(8,128)(2,1)} %bitcast.6, bf16[4,1280,640]{2,1,0:T(8,128)(2,1)} %spw_h.1, f32[1280]{0:T(1024)} %spg.1, bf16[4,160,640]{2,1,0:T(8,128)(2,1)} %mw_h.1, ...), custom_call_target="tpu_custom_call" | custom-call | tf_op jit(solution)/shard_map/pallas_call | solution.py:715
  93.6 3.1 %shard_map.112 = (bf16[128,1280]{1,0:T(8,128)(2,1)}, bf16[128,1280]{1,0:T(8,128)(2,1)}, f32[5,4,640]{2,1,0:T(4,128)}, f32[5]{0:T(128)}) custom-call(bf16[128,1280]{1,0:T(8,128)(2,1)} %get-tuple-element.12.bo_h, bf16[128,1280]{1,0:T(8,128)(2,1)} %get-tuple-element.13.ig_h, f32[5,4,640]{2,1,0:T(4,128)} %get-tuple-element.14.wg_h, f32[1,1280]{1,0:T(1,128)} %get-tuple-element.15.gn), custom_call_target="tpu_custom_call" | custom-call | tf_op jit(solution)/shard_map/pallas_call | solution.py:727

commit v6 on v5

--- a/solution.py
+++ b/solution.py
@@ -22,9 +22,10 @@
     (0, 0, 256, (XB, ZA)),
     (0, 256, 256, (YA, ZB)),
     (0, 512, 128, (YB, ZA)),
-    (1, 0, 256, (XA, ZB)),
-    (1, 256, 256, (YB, ZA)),
-    (1, 512, 128, (XB, ZB)),
+    (1, 0, 128, (XA, YA)),
+    (1, 128, 256, (YB, XB)),
+    (1, 384, 128, (XB, YB)),
+    (1, 512, 128, (YA, XA)),
 )
 MESH = pl.DeviceIdType.MESH
 
@@ -104,8 +105,8 @@
 
 
 def kernel(act_h, cot_h, spw_h, spg, mw_h, mgn, pe_h, perm_h,
-           bo_h, ig_h, wg, gn,
-           act, cot, spw, spt, mw, pe, perm, bo, ig,
+           bo_h, ig_h, wg_h,
+           act, cot, spw, spt, mw, pe, perm, bo, ig, wg,
            qkv_s, qkv_r, o_s, o_r, prob_s,
            hid, hid_s, hid_r, ct_s, ct_r, ctt, tx, n2s, u2s, r2s, mqkv, prob_t,
            mo_s, mo_r, lb_s, lb_r, gh, mof,
@@ -179,6 +180,9 @@
     @pl.loop(1, 8)
     def _(d):
         pl.semaphore_signal(bar, inc=1, device_id=((1 - x_lo) * 16 + zc, qpeer(d)), device_id_type=MESH)
+        for n in range(2):
+            near = n * 16 + z // 2 * 4 + (1 - even) * 2 + core
+            pl.semaphore_signal(bar, inc=1, device_id=(near, qpeer(d)), device_id_type=MESH)
 
     loads[0].wait()
     u1, _ = unit(act[...].astype(F32))
@@ -187,7 +191,7 @@
         loads[1 + t].wait()
         for hp, part in enumerate(split_pair(nn(n1, spw[t]))):
             qkv_s[hp * 4:hp * 4 + 4, t] = part.astype(BF).reshape(4, 32, 384)
-    pl.semaphore_wait(bar, 45)
+    pl.semaphore_wait(bar, 59)
 
     def q_copy(d):
         return remote(qkv_s.at[qpeer(d)], qkv_r.at[j], q_ss.at[0], q_rs.at[0], (i, qpeer(d)))
@@ -298,11 +302,11 @@
     for c in wz:
         c.start()
     wy_start(1)
+    w2_pass(0)
+
+    arrived(o_r.at[0:7], o_ss.at[0], o_rs.at[0])
+
     w1_start(3)
-    w2_pass(0)
-
-    arrived(o_r.at[0:7], o_ss.at[0], o_rs.at[0])
-
     wy_start(3)
     so = join_pair(o_r[0:4].reshape(128, 384).astype(F32), o_r[4:8].reshape(128, 384).astype(F32)).astype(BF)
     hid[...] = (act[...].astype(F32) + nn(so, spt[3])).astype(BF)
@@ -461,15 +465,15 @@
     def direct(p):
         digits = left(p, 2)
         for mask in range(1, 8):
-            to = [own[n] for n in range(4)]
+            to = list(own)
             for bit, n in enumerate(digits):
                 if mask >> bit & 1:
                     to[n] = 1 - own[n]
             ref, at = block(p, 2, {n: to[n] for n in digits})
-            device = ((to[0] + to[1]) % 2 * 16 + zc, to[0] * 4 + to[2] * 2 + (to[2] + to[3]) % 2)
+            device = ((to[0] + to[1]) % 2 * 16 + z // 2 * 4 + to[4] * 2 + core, to[0] * 4 + to[2] * 2 + (to[2] + to[3]) % 2)
             remote(ref.at[at], buffers[6 * p + 4].at[mask - 1], p_ss.at[3 * p + 2], p_rs.at[3 * p + 2], device).start()
 
-    done = [0] * 6
+    done = [0] * 7
 
     def begin(p):
         step_copy(p, 0).start()
@@ -523,7 +527,7 @@
     swap_b.wait()
     wb[...] = tn(ax[1], ay[1]).reshape(2, 2, 2, 2, 2, 40, W).astype(BF)
 
-    for p in (3, 4, 5):
+    for p in (3, 4, 5, 6):
         begin(p)
 
     arrived(mo_r.at[0:31], m_ss.at[0], m_rs.at[0])
@@ -559,20 +563,23 @@
     gy = [v_copy(gv2, gr2.at[d - 1], 1, ypeer(d)) for d in range(1, 4)]
     for c in gy:
         c.start()
+    advance(5)
+    advance(6)
     advance(4)
-    advance(5)
     advance(3)
     arrived(gs_r.at[0:7], gs_ss.at[0], gs_rs.at[0])
     advance(2)
     advance(0)
     advance(1)
-    advance(4)
-    advance(5)
-    advance(3)
 
     q, k, v = (qkv_r[:, t].reshape(256, 384) for t in range(3))
     for t, grad in enumerate(attend_back(q, k, v, gs_r[...].reshape(256, 384), prob_s, 2)):
         dq_s[:, t] = grad.astype(BF).reshape(8, 32, 384)
+
+    advance(5)
+    advance(6)
+    advance(3)
+    advance(4)
 
     def dq_copy(d):
         return remote(dq_s.at[qpeer(d)], dq_r.at[j], dq_ss.at[0], dq_rs.at[0], (i, qpeer(d)))
@@ -595,7 +602,7 @@
     gz.wait()
     gv = gv3[...] + gr3[...]
     sum_a = jnp.concatenate([result(p) for p in (0, 1, 2)], axis=1)
-    sum_b = jnp.concatenate([result(p) for p in (3, 4, 5)], axis=1)
+    sum_b = jnp.concatenate([result(p) for p in (3, 4, 5, 6)], axis=1)
     slabs = nn(first, sum_a) + nn(second, sum_b)
     row = lax.broadcasted_iota(jnp.int32, (128, W), 0) % 16
     slabs = jnp.where(row == 10, gv[:, :W], jnp.where(row == 11, gv[:, W:], slabs))
@@ -634,27 +641,33 @@
         for n in range(1, 4):
             total = total + r3[2 * n + c].astype(F32)
         sums.append(total * factor)
-    wg[:, 0] = sums[0][5:10]
-    wg[:, 1] = sums[1][5:10]
-    wg[:, 2] = sums[1][0:5]
-    wg[:, 3] = sums[0][0:5]
-    both = sums[0] + sums[1]
-    gn[...] = jnp.concatenate([both[10:11], both[11:12]], axis=1)
+    wg[0:5, 0] = sums[0][5:10]
+    wg[0:5, 1] = sums[1][5:10]
+    wg[0:5, 2] = sums[1][0:5]
+    wg[0:5, 3] = sums[0][0:5]
+    wg[5, 0:2] = (sums[0] + sums[1])[10:12]
+    wg_store = pltpu.make_async_copy(wg, wg_h, st.at[2])
+    wg_store.start()
+    wg_store.wait()
     bo_store.wait()
     ig_store.wait()
 
 
-def finish(bo_h, ig_h, wg_h, gn, bo, ig, wg, gg, bo_v, ig_v, wg_v, sems):
-    moves = [(bo_h, bo_v, bo), (ig_h, ig_v, ig), (wg_h, wg_v, wg)]
-    come = [pltpu.make_async_copy(a, b, sems.at[0, n]) for n, (a, b, _) in enumerate(moves)]
-    go = [pltpu.make_async_copy(b, c, sems.at[1, n]) for n, (_, b, c) in enumerate(moves)]
+def finish(bo_h, ig_h, wg_h, bo, ig, wg, gg, bo_v, ig_v, wg_v, sems):
+    rows = [pl.ds(32 * n, 32) for n in range(4)]
+    moves = [(wg_h, wg_v, wg_v.at[0:5], wg)]
+    for r in rows:
+        moves += [(bo_h.at[r], bo_v.at[r], bo_v.at[r], bo.at[r]), (ig_h.at[r], ig_v.at[r], ig_v.at[r], ig.at[r])]
+    come = [pltpu.make_async_copy(a, b, sems.at[0, n]) for n, (a, b, _, _) in enumerate(moves)]
+    go = [pltpu.make_async_copy(c, d, sems.at[1, n]) for n, (_, _, c, d) in enumerate(moves)]
     for c in come:
         c.start()
-    device = lax.axis_index("frame") * 8 + lax.axis_index("quad")
-    gg[...] = pltpu.roll(gn[...], C - device * 5, 1)[0, :5]
     for a, b in zip(come, go):
         a.wait()
         b.start()
+    device = lax.axis_index("frame") * 8 + lax.axis_index("quad")
+    gain = jnp.concatenate([wg_v[5, 0:1, :], wg_v[5, 1:2, :]], axis=1)
+    gg[...] = pltpu.roll(gain, C - device * 5, 1)[0, :5]
     for c in go:
         c.wait()
 
@@ -694,7 +707,7 @@
     any_, vmem = pl.BlockSpec(memory_space=pl.ANY), pl.BlockSpec(memory_space=pltpu.VMEM)
     scratch = [
         V((128, C), BF), V((128, C), BF), V((4, C, W), BF), V((4, W, C), BF), V((4, 8, 160, W), BF), V((128, C), F32), V((C, C), BF),
-        V((128, C), BF), V((128, C), BF),
+        V((128, C), BF), V((128, C), BF), V((6, 4, W), F32),
         V((8, 3, 32, 384), BF), V((8, 3, 32, 384), BF), V((8, 32, 384), BF), V((8, 32, 384), BF), V((2, 256, 256), F32),
         V((128, C), BF), V((32, 4, C), BF), V((32, 4, C), BF), V((32, 4, C), BF), V((32, 4, C), BF), V((128, C), BF),
         V((128, C), F32), V((128, C), BF), V((128, C), F32), V((128, 128), F32), V((3, 128, W), BF), V((4, 128, 128), F32),
@@ -703,20 +716,16 @@
         V((2, 128, C), BF), V((2, 128, W), BF), V((2, 256, C), BF), V((2, 256, W), BF),
         V((2, 2, 2, 2, 2, 40, W), BF), V((2, 2, 2, 2, 2, 40, W), BF), V((8, 16, W), BF), V((8, 16, W), BF),
         V((1, C), F32), V((3, 1, C), F32), V((1, C), F32), V((3, 1, C), F32), V((1, C), F32), V((1, C), F32),
-        D((10,)), D((2,))] + [D((4,))] * 14 + [D((1,))] * 16 + [
-        D((4,)), D((4,)), D((18,)), D((18,)), D((1,)), D((1,)),
+        D((10,)), D((3,))] + [D((4,))] * 14 + [D((1,))] * 16 + [
+        D((4,)), D((4,)), D((21,)), D((21,)), D((1,)), D((1,)),
         D((3,)), D((3,)),
     ] + part_buffers()
-    results = (
-        jax.ShapeDtypeStruct((128, C), BF),
-        jax.ShapeDtypeStruct((128, C), BF),
-        jax.ShapeDtypeStruct((5, 4, W), F32),
-    )
-    block_output, input_grad, weight_grad, gain_all = pl.pallas_call(
+    tokens = jax.ShapeDtypeStruct((128, C), BF)
+    block_output, input_grad, sums = pl.pallas_call(
         kernel,
-        out_shape=results + (jax.ShapeDtypeStruct((1, C), F32),),
+        out_shape=(tokens, tokens, jax.ShapeDtypeStruct((6, 4, W), F32)),
         in_specs=[any_, any_, any_, vmem, any_, vmem, any_, any_],
-        out_specs=(any_, any_, vmem, vmem),
+        out_specs=(any_, any_, any_),
         scratch_shapes=scratch,
         compiler_params=pltpu.CompilerParams(
             has_side_effects=True, collective_id=0, vmem_limit_bytes=60 * 2 ** 20),
@@ -726,12 +735,12 @@
     )
     block_output, input_grad, weight_grad, gain_grad = pl.pallas_call(
         finish,
-        out_shape=results + (jax.ShapeDtypeStruct((5,), F32),),
-        in_specs=[any_, any_, any_, vmem],
+        out_shape=(tokens, tokens, jax.ShapeDtypeStruct((5, 4, W), F32), jax.ShapeDtypeStruct((5,), F32)),
+        in_specs=[any_, any_, any_],
         out_specs=(any_, any_, any_, vmem),
-        scratch_shapes=[V((128, C), BF), V((128, C), BF), V((5, 4, W), F32), D((2, 3))],
+        scratch_shapes=[V((128, C), BF), V((128, C), BF), V((6, 4, W), F32), D((2, 9))],
         compiler_params=pltpu.CompilerParams(vmem_limit_bytes=60 * 2 ** 20),
-    )(block_output, input_grad, weight_grad, gain_all)
+    )(block_output, input_grad, sums)
     shape = activations.shape
     return block_output.reshape(shape), input_grad.reshape(shape), weight_grad.transpose(1, 0, 2), gain_grad
 

time: 97.7 us -> 96.3 us (0.986)
  no operation moved by 1% of the time
where the time goes in v6:
time: 96.3 us; the launch traced here: 96.2 us
  Pallas kernels  95.4 us (99%)
    pallas_call x1, Pallas kernels, local(): pl.pallas_call(kernel, out_shape=(tokens, tokens, jax.ShapeDtypeStruct((6...  92.9 us
    pallas_call x1, Pallas kernels, local(): pl.pallas_call(finish, out_shape=(tokens, tokens, jax.ShapeDtypeStruct((5...  2.49 us

profile of v6, /device:TPU:1, one launch (start us, length us, event | category | flops | bytes accessed | tf_op | source)
XLA Modules:
  0.0 96.2 jit_solution(6010869020820593845)
XLA Ops:
  0.6 92.9 %shard_map.111 = (bf16[128,1280]{1,0:T(8,128)(2,1)}, bf16[128,1280]{1,0:T(8,128)(2,1)}, f32[6,4,640]{2,1,0:T(4,128)}) custom-call(bf16[128,1280]{1,0:T(8,128)(2,1)} %bitcast.5, bf16[128,1280]{1,0:T(8,128)(2,1)} %bitcast.6, bf16[4,1280,640]{2,1,0:T(8,128)(2,1)} %spw_h.1, f32[1280]{0:T(1024)} %spg.1, bf16[4,160,640]{2,1,0:T(8,128)(2,1)} %mw_h.1, f32[1280]{0:T(1024)} %mgn.1, ...), custom_call_target="tpu_custom_call" | custom-call | tf_op jit(solution)/shard_map/pallas_call | solution.py:724
  93.5 2.5 %shard_map.112 = (bf16[128,1280]{1,0:T(8,128)(2,1)}, bf16[128,1280]{1,0:T(8,128)(2,1)}, f32[5,4,640]{2,1,0:T(4,128)}, f32[5]{0:T(128)}) custom-call(bf16[128,1280]{1,0:T(8,128)(2,1)} %get-tuple-element.11.bo_h, bf16[128,1280]{1,0:T(8,128)(2,1)} %get-tuple-element.12.ig_h, f32[6,4,640]{2,1,0:T(4,128)} %get-tuple-element.13.wg_h), custom_call_target="tpu_custom_call" | custom-call | tf_op jit(solution)/shard_map/pallas_call | solution.py:736

commit v7 on v6

--- a/solution.py
+++ b/solution.py
@@ -208,11 +208,11 @@
 
     def w2_copy(n):
         part = mw.at[matrix[n], pl.ds(x_hi * 4 + 2 * (1 - x_lo), 2), half]
-        return remote(part, part, w2_ss.at[n], w2_rs.at[n], cross)
+        return remote(part, part, w2_ss.at[n // 2], w2_rs.at[n // 2], cross)
 
     def w3_copy(n):
         part = mw.at[matrix[n], pl.ds((1 - x_hi) * 4 + 2 * x_lo, 2), half]
-        return remote(part, part, w3_ss.at[n], w3_rs.at[n], beside)
+        return remote(part, part, w3_ss.at[n // 2], w3_rs.at[n // 2], beside)
 
     def w4_copy(n):
         part = mw.at[matrix[n], :, half]
@@ -224,11 +224,11 @@
 
     def wx_copy(n):
         m = matrix[n]
-        return remote(mw_h.at[m, half], mw.at[m, j, half], wx_ss.at[n], wx_rs.at[n], cross)
+        return remote(mw_h.at[m, half], mw.at[m, j, half], wx_ss.at[n // 2], wx_rs.at[n // 2], cross)
 
     def wy_copy(n, d):
         part = mw.at[matrix[n], (1 - x_hi) * 4 + y, half]
-        return remote(part, part, wy_ss.at[n], wy_rs.at[n], ypeer(d))
+        return remote(part, part, wy_ss.at[n // 2], wy_rs.at[n // 2], ypeer(d))
 
     def w1_start(n):
         for d in (1, 3, 2):
@@ -243,7 +243,7 @@
             wy_copy(n, d).start()
 
     def wy_pass(n):
-        arrived(mw.at[matrix[n], 0:3, half], wy_ss.at[n], wy_rs.at[n])
+        arrived(mw.at[matrix[n], 0:3, half], wy_ss.at[n // 2], wy_rs.at[n // 2])
         w4_copy(n).start()
 
     def w2_pass(n):
@@ -567,10 +567,10 @@
     advance(6)
     advance(4)
     advance(3)
-    arrived(gs_r.at[0:7], gs_ss.at[0], gs_rs.at[0])
     advance(2)
     advance(0)
     advance(1)
+    arrived(gs_r.at[0:7], gs_ss.at[0], gs_rs.at[0])
 
     q, k, v = (qkv_r[:, t].reshape(256, 384) for t in range(3))
     for t, grad in enumerate(attend_back(q, k, v, gs_r[...].reshape(256, 384), prob_s, 2)):
@@ -667,7 +667,7 @@
         b.start()
     device = lax.axis_index("frame") * 8 + lax.axis_index("quad")
     gain = jnp.concatenate([wg_v[5, 0:1, :], wg_v[5, 1:2, :]], axis=1)
-    gg[...] = pltpu.roll(gain, C - device * 5, 1)[0, :5]
+    gg[...] = pltpu.roll(gain, (C - device * 5) % C, 1)[0, :5]
     for c in go:
         c.wait()
 
@@ -716,7 +716,7 @@
         V((2, 128, C), BF), V((2, 128, W), BF), V((2, 256, C), BF), V((2, 256, W), BF),
         V((2, 2, 2, 2, 2, 40, W), BF), V((2, 2, 2, 2, 2, 40, W), BF), V((8, 16, W), BF), V((8, 16, W), BF),
         V((1, C), F32), V((3, 1, C), F32), V((1, C), F32), V((3, 1, C), F32), V((1, C), F32), V((1, C), F32),
-        D((10,)), D((3,))] + [D((4,))] * 14 + [D((1,))] * 16 + [
+        D((10,)), D((3,))] + [D((4,))] * 2 + [D((2,))] * 4 + [D((4,))] * 2 + [D((2,))] * 6 + [D((1,))] * 16 + [
         D((4,)), D((4,)), D((21,)), D((21,)), D((1,)), D((1,)),
         D((3,)), D((3,)),
     ] + part_buffers()

time: 96.3 us -> 95.1 us (0.988)
  Pallas kernels: 95.4 us -> 94.1 us
    pallas_call x1, Pallas kernels: 92.9 us -> 91.6 us  [local(): pl.pallas_call(kernel, out_shape=(tokens, tokens, jax.ShapeDtypeStruct((6...]
where the time goes in v7:
time: 95.1 us; the launch traced here: 94.9 us
  Pallas kernels  94.1 us (99%)
    pallas_call x1, Pallas kernels, local(): pl.pallas_call(kernel, out_shape=(tokens, tokens, jax.ShapeDtypeStruct((6...  91.6 us
    pallas_call x1, Pallas kernels, local(): pl.pallas_call(finish, out_shape=(tokens, tokens, jax.ShapeDtypeStruct((5...  2.49 us

profile of v7, /device:TPU:1, one launch (start us, length us, event | category | flops | bytes accessed | tf_op | source)
XLA Modules:
  0.0 94.9 jit_solution(18164265508706108547)
XLA Ops:
  0.6 91.6 %shard_map.111 = (bf16[128,1280]{1,0:T(8,128)(2,1)}, bf16[128,1280]{1,0:T(8,128)(2,1)}, f32[6,4,640]{2,1,0:T(4,128)}) custom-call(bf16[128,1280]{1,0:T(8,128)(2,1)} %bitcast.5, bf16[128,1280]{1,0:T(8,128)(2,1)} %bitcast.6, bf16[4,1280,640]{2,1,0:T(8,128)(2,1)} %spw_h.1, f32[1280]{0:T(1024)} %spg.1, bf16[4,160,640]{2,1,0:T(8,128)(2,1)} %mw_h.1, f32[1280]{0:T(1024)} %mgn.1, ...), custom_call_target="tpu_custom_call" | custom-call | tf_op jit(solution)/shard_map/pallas_call | solution.py:724
  92.3 2.5 %shard_map.112 = (bf16[128,1280]{1,0:T(8,128)(2,1)}, bf16[128,1280]{1,0:T(8,128)(2,1)}, f32[5,4,640]{2,1,0:T(4,128)}, f32[5]{0:T(128)}) custom-call(bf16[128,1280]{1,0:T(8,128)(2,1)} %get-tuple-element.11.bo_h, bf16[128,1280]{1,0:T(8,128)(2,1)} %get-tuple-element.12.ig_h, f32[6,4,640]{2,1,0:T(4,128)} %get-tuple-element.13.wg_h), custom_call_target="tpu_custom_call" | custom-call | tf_op jit(solution)/shard_map/pallas_call | solution.py:736

commit v8 on v7

--- a/solution.py
+++ b/solution.py
@@ -620,6 +620,7 @@
 
     r3[place] = p3[place]
 
+    u1, r1 = unit(act[...].astype(F32))
     arrived(dq_r.at[0:7], dq_ss.at[0], dq_rs.at[0])
 
     total = None
@@ -627,7 +628,6 @@
         grad = join_pair(dq_r[0:4, t].reshape(128, 384).astype(F32), dq_r[4:8, t].reshape(128, 384).astype(F32)).astype(BF)
         term = nn(grad, spt[t])
         total = term if total is None else total + term
-    u1, r1 = unit(act[...].astype(F32))
     ig[...] = (gh[...].astype(F32) + unit_back(total, u1, r1, spg[...].reshape(1, C))).astype(BF)
     ig_store = pltpu.make_async_copy(ig, ig_h, st.at[1])
     ig_store.start()

time: 95.1 us -> 95.1 us (level)
  no operation moved by 1% of the time
where the time goes in v8:
time: 95.1 us; the launch traced here: 94.9 us
  Pallas kernels  94.1 us (99%)
    pallas_call x1, Pallas kernels, local(): pl.pallas_call(kernel, out_shape=(tokens, tokens, jax.ShapeDtypeStruct((6...  91.6 us
    pallas_call x1, Pallas kernels, local(): pl.pallas_call(finish, out_shape=(tokens, tokens, jax.ShapeDtypeStruct((5...  2.49 us

profile of v8, /device:TPU:1, one launch (start us, length us, event | category | flops | bytes accessed | tf_op | source)
XLA Modules:
  0.0 94.9 jit_solution(5194180967381921358)
XLA Ops:
  0.6 91.6 %shard_map.111 = (bf16[128,1280]{1,0:T(8,128)(2,1)}, bf16[128,1280]{1,0:T(8,128)(2,1)}, f32[6,4,640]{2,1,0:T(4,128)}) custom-call(bf16[128,1280]{1,0:T(8,128)(2,1)} %bitcast.5, bf16[128,1280]{1,0:T(8,128)(2,1)} %bitcast.6, bf16[4,1280,640]{2,1,0:T(8,128)(2,1)} %spw_h.1, f32[1280]{0:T(1024)} %spg.1, bf16[4,160,640]{2,1,0:T(8,128)(2,1)} %mw_h.1, f32[1280]{0:T(1024)} %mgn.1, ...), custom_call_target="tpu_custom_call" | custom-call | tf_op jit(solution)/shard_map/pallas_call | solution.py:724
  92.3 2.5 %shard_map.112 = (bf16[128,1280]{1,0:T(8,128)(2,1)}, bf16[128,1280]{1,0:T(8,128)(2,1)}, f32[5,4,640]{2,1,0:T(4,128)}, f32[5]{0:T(128)}) custom-call(bf16[128,1280]{1,0:T(8,128)(2,1)} %get-tuple-element.11.bo_h, bf16[128,1280]{1,0:T(8,128)(2,1)} %get-tuple-element.12.ig_h, f32[6,4,640]{2,1,0:T(4,128)} %get-tuple-element.13.wg_h), custom_call_target="tpu_custom_call" | custom-call | tf_op jit(solution)/shard_map/pallas_call | solution.py:736
